TPU v7x, 256 devices: a whole 4x4x8 slice. The times are simulated.
256 devices in a mesh: inst: 16 (over x, y_hi, core), tp: 16 (over z, y_lo).
Axes of the slice: x: 4, y: 4 (y_hi: 2, y_lo: 2; y = y_hi * 2 + y_lo), z: 8, core: 2. Of those that a mesh axis runs over, the one named last changes fastest.
Arguments:
- fresh_segment_probes: bfloat16 [4096, 64, 128], P('inst', 'tp'), may hold values from -10 to 10
- fresh_segment_pairs: bfloat16 [4096, 2, 16, 128], P('inst', None, 'tp'), may hold values from -5 to 5
- earlier_stored_pairs: bfloat16 [16384, 2, 16, 128], P('inst', None, 'tp'), may hold values from -5 to 5
- emitted_token_probe: bfloat16 [64, 128], P('tp'), may hold values from -10 to 10
- emitted_token_pair: bfloat16 [2, 16, 128], P(None, 'tp'), may hold values from -5 to 5
- final_projection_weights: bfloat16 [8192, 8192], P('tp', 'inst'), may hold values from -0.0625 to 0.0625
- remaining_instance_ids: int32 [8], replicated, may hold values from 0 to 15, as said below
- segment_destination_member: int32 [32, 1], replicated, may hold values from 0 to 7; in each aligned block of 32 rows (0 to 31, 32 to 63, ...) at most 8 rows name the same one
Outputs:
- span_hidden: bfloat16 [4096, 8192], P('inst', 'tp')
- migrated_cache: bfloat16 [16, 1024, 2, 16, 128], P('inst', None, None, 'tp')
- decode_attention: bfloat16 [64, 128], P('tp')
Inputs may be any that keep to these rules, and one draw needn't show every extreme that they name: `segment_destination_member`: at most 8 blocks name one survivor, a bound that some block reaches. `remaining_instance_ids`: 8 distinct instance indices; instances 0 and 15 always survive.
All inputs are finite; a program needn't handle non-finite values.
Results may differ from a plain program's by a relative error of at most 0.024.
Values may be sent and summed in bfloat16 or wider, within the bound.
A program may use at most 128 MiB of HBM per device.

v0:
```python
import jax
import jax.numpy as jnp
from jax import lax
from jax.sharding import PartitionSpec as P

BLK = 128
CAP = 8


NEG_FILL = -1e30


def from_behind(block, axis, distance):
    devices = range(lax.axis_size(axis))
    route = [((i - distance) % len(devices), i) for i in devices]
    return lax.ppermute(block, axis, route)


def combined_all(value, axis, combine):
    everything = jax.tree.map(lambda part: lax.all_gather(part, axis), value)
    initial = jax.tree.map(lambda part: part[0], everything)

    def turn(k, so_far):
        return combine(so_far, jax.tree.map(lambda part: part[k], everything))

    return lax.fori_loop(1, lax.axis_size(axis), turn, initial)


def attend(state, queries, key_value, visible):
    width = queries.shape[-1]
    scores = jnp.einsum(
        "rkgd,nkd->rkgn", queries, key_value[:, 0], preferred_element_type=jnp.float32
    ) * width ** (-0.5)
    if visible is not None:
        scores = jnp.where(visible[:, None, None, :], scores, NEG_FILL)
    running, total, weighted = state
    highest = jnp.maximum(running, jnp.max(scores, axis=-1))
    factor = jnp.exp(running - highest)
    weights = jnp.exp(scores - highest[..., None])
    total = total * factor + jnp.sum(weights, axis=-1)
    update = jnp.einsum(
        "rkgn,nkd->rkgd",
        weights.astype(jnp.bfloat16),
        key_value[:, 1],
        preferred_element_type=jnp.float32,
    )
    weighted = weighted * factor[..., None] + update
    return (highest, total, weighted)


def empty_state(rows, slots_local, group, width):
    return (
        jnp.full((rows, slots_local, group), -jnp.inf, jnp.float32),
        jnp.zeros((rows, slots_local, group), jnp.float32),
        jnp.zeros((rows, slots_local, group, width), jnp.float32),
    )


def combine(first, second):
    highest = jnp.maximum(first[0], second[0])
    left = jnp.exp(first[0] - highest)
    right = jnp.exp(second[0] - highest)
    return (
        highest,
        first[1] * left + second[1] * right,
        first[2] * left[..., None] + second[2] * right[..., None],
    )


def place_blocks(cache, rows_in, destination_members, slots, own_index):
    count = rows_in.shape[0] // BLK

    def put(index, current):
        spot = slots[index] * BLK
        incoming = lax.dynamic_slice_in_dim(rows_in, index * BLK, BLK, 0)
        present = lax.dynamic_slice_in_dim(current, spot, BLK, 0)
        chosen = jnp.where(destination_members[index] == own_index, incoming, present)
        return lax.dynamic_update_slice_in_dim(current, chosen, spot, 0)

    return lax.fori_loop(0, count, put, cache)


def on_device(
    fresh_segment_probes,
    fresh_segment_pairs,
    earlier_stored_pairs,
    emitted_token_probe,
    emitted_token_pair,
    final_projection_weights,
    remaining_instance_ids,
    segment_destination_member,
):
    own_index = lax.axis_index("inst")
    instances = lax.axis_size("inst")
    rows, heads, width = fresh_segment_probes.shape
    slots_local = fresh_segment_pairs.shape[2]
    group = heads // slots_local
    queries = fresh_segment_probes.reshape(rows, slots_local, group, width)
    destination_sequence = segment_destination_member[:, 0]
    destination_agreement = (
        destination_sequence[:, None]
        == jnp.arange(remaining_instance_ids.shape[0], dtype=jnp.int32)[None, :]
    ).astype(jnp.int32)
    slots = jnp.sum(jnp.cumsum(destination_agreement, axis=0) * destination_agreement, axis=1) - 1
    destination_members = jnp.sum(destination_agreement * remaining_instance_ids[None, :], axis=1)
    held_blocks = jnp.sum((destination_members == own_index).astype(jnp.int32))
    cache = jnp.zeros((CAP * BLK, 2, slots_local, width), jnp.bfloat16)
    causal = jnp.arange(rows)[:, None] >= jnp.arange(rows)[None, :]
    state = attend(
        empty_state(rows, slots_local, group, width), queries, earlier_stored_pairs, None
    )
    state = attend(state, queries, fresh_segment_pairs, causal)
    moving = jnp.concatenate([fresh_segment_pairs, earlier_stored_pairs], axis=0)

    def turn_both(step, carry):
        moving, state, current = carry
        moving = from_behind(moving, "inst", 1)
        source = (own_index - step) % instances
        state = attend(state, queries, moving[rows:], None)
        visible = jnp.broadcast_to(source < own_index, (rows, rows))
        state = attend(state, queries, moving[:rows], visible)
        return (moving, state, current)

    moving, state, cache = lax.fori_loop(1, instances, turn_both, (moving, state, cache))
    cache = place_blocks(
        cache,
        lax.all_gather(fresh_segment_pairs, "inst", axis=0, tiled=True),
        destination_members,
        slots,
        own_index,
    )
    attention = (state[2] / state[1][..., None]).astype(jnp.bfloat16).reshape(rows, heads * width)
    terms = jnp.dot(
        attention,
        lax.all_gather(final_projection_weights, "inst", axis=1, tiled=True),
        preferred_element_type=jnp.float32,
    )
    span_hidden = lax.psum_scatter(
        terms.astype(jnp.bfloat16), "tp", scatter_dimension=1, tiled=True
    )
    single = emitted_token_probe.reshape(1, slots_local, group, width)
    decode_state = attend(
        empty_state(1, slots_local, group, width), single, earlier_stored_pairs, None
    )
    live = (jnp.arange(CAP * BLK) < held_blocks * BLK)[None, :]
    decode_state = attend(decode_state, single, cache, live)
    merged = combined_all((decode_state[0], decode_state[1], decode_state[2]), "inst", combine)
    own_scores = jnp.einsum(
        "rkgd,kd->rkg", single, emitted_token_pair[0], preferred_element_type=jnp.float32
    ) * width ** (-0.5)
    highest = jnp.maximum(merged[0], own_scores)
    left = jnp.exp(merged[0] - highest)
    right = jnp.exp(own_scores - highest)
    total = merged[1] * left + right
    own_weight = lax.optimization_barrier(right.astype(jnp.bfloat16)).astype(jnp.float32)
    own_value = emitted_token_pair[1].astype(jnp.float32)
    weighted = merged[2] * left[..., None] + own_weight[..., None] * own_value[None, :, None, :]
    decode_attention = (weighted / total[..., None]).astype(jnp.bfloat16).reshape(heads, width)
    return (span_hidden, cache[None], decode_attention)


def solution(mesh):
    return jax.shard_map(
        on_device,
        mesh=mesh,
        in_specs=(
            P("inst", "tp", None),
            P("inst", None, "tp", None),
            P("inst", None, "tp", None),
            P("tp", None),
            P(None, "tp", None),
            P("tp", "inst"),
            P(),
            P(),
        ),
        out_specs=(P("inst", "tp"), P("inst", None, None, "tp", None), P("tp", None)),
        check_vma=False,
    )
```

profile of v0, /device:TPU:2, one launch (start us, length us, event | category | flops | bytes accessed | tf_op | source)
XLA Modules:
  0.0 595.5 jit_solution(17190623237007363333)
XLA Ops:
  10.9 3.6 bitcast_reduce_fusion.1
  18.3 3.3 fusion.65
  21.6 262.6 %while.53 = (s32[]{:T(128)}, bf16[1280,2,1,128]{3,0,2,1:T(8,128)(2,1)S(1)}, f32[256,1,4]{0,2,1:T(4,128)S(1)}, f32[256,1,4]{0,2,1:T(4,128)S(1)}, f32[256,1,4,128]...) while((s32[]{:T(128)}, ...), condition=%wide.region_9.10_spmd, body=%wide.region_4.9_spmd.sunk | while | flops 681843712 | bytes 23044376 | solution.py:124
  21.7 13.3 %collective-permute-done = bf16[1280,2,1,128]{3,0,2,1:T(8,128)(2,1)S(1)} collective-permute-done((bf16[1280,2,1,128]{3,0,2,1:T(8,128)(2,1)S(1)}, bf16[1280,2,1,128]{3,0,2,1:T(8,128)(2,1)S(1)}, u32[]{:S(2)}, u32[]{:S(2)}) %collective-permute-start) | collective-permute-done | bytes 655392 | tf_op jit(solution)/shard_map/while/body/eval_jaxpr/ppermute | solution.py:16
  38.8 12.4 %collective-permute-done = bf16[1280,2,1,128]{3,0,2,1:T(8,128)(2,1)S(1)} collective-permute-done((bf16[1280,2,1,128]{3,0,2,1:T(8,128)(2,1)S(1)}, bf16[1280,2,1,128]{3,0,2,1:T(8,128)(2,1)S(1)}, u32[]{:S(2)}, u32[]{:S(2)}) %collective-permute-start) | collective-permute-done | bytes 655392 | tf_op jit(solution)/shard_map/while/body/eval_jaxpr/ppermute | solution.py:16
  54.9 14.5 %collective-permute-done = bf16[1280,2,1,128]{3,0,2,1:T(8,128)(2,1)S(1)} collective-permute-done((bf16[1280,2,1,128]{3,0,2,1:T(8,128)(2,1)S(1)}, bf16[1280,2,1,128]{3,0,2,1:T(8,128)(2,1)S(1)}, u32[]{:S(2)}, u32[]{:S(2)}) %collective-permute-start) | collective-permute-done | bytes 655392 | tf_op jit(solution)/shard_map/while/body/eval_jaxpr/ppermute | solution.py:16
  73.2 12.4 %collective-permute-done = bf16[1280,2,1,128]{3,0,2,1:T(8,128)(2,1)S(1)} collective-permute-done((bf16[1280,2,1,128]{3,0,2,1:T(8,128)(2,1)S(1)}, bf16[1280,2,1,128]{3,0,2,1:T(8,128)(2,1)S(1)}, u32[]{:S(2)}, u32[]{:S(2)}) %collective-permute-start) | collective-permute-done | bytes 655392 | tf_op jit(solution)/shard_map/while/body/eval_jaxpr/ppermute | solution.py:16
  89.3 18.0 %collective-permute-done = bf16[1280,2,1,128]{3,0,2,1:T(8,128)(2,1)S(1)} collective-permute-done((bf16[1280,2,1,128]{3,0,2,1:T(8,128)(2,1)S(1)}, bf16[1280,2,1,128]{3,0,2,1:T(8,128)(2,1)S(1)}, u32[]{:S(2)}, u32[]{:S(2)}) %collective-permute-start) | collective-permute-done | bytes 655392 | tf_op jit(solution)/shard_map/while/body/eval_jaxpr/ppermute | solution.py:16
  111.1 18.0 %collective-permute-done = bf16[1280,2,1,128]{3,0,2,1:T(8,128)(2,1)S(1)} collective-permute-done((bf16[1280,2,1,128]{3,0,2,1:T(8,128)(2,1)S(1)}, bf16[1280,2,1,128]{3,0,2,1:T(8,128)(2,1)S(1)}, u32[]{:S(2)}, u32[]{:S(2)}) %collective-permute-start) | collective-permute-done | bytes 655392 | tf_op jit(solution)/shard_map/while/body/eval_jaxpr/ppermute | solution.py:16
  132.8 12.5 %collective-permute-done = bf16[1280,2,1,128]{3,0,2,1:T(8,128)(2,1)S(1)} collective-permute-done((bf16[1280,2,1,128]{3,0,2,1:T(8,128)(2,1)S(1)}, bf16[1280,2,1,128]{3,0,2,1:T(8,128)(2,1)S(1)}, u32[]{:S(2)}, u32[]{:S(2)}) %collective-permute-start) | collective-permute-done | bytes 655392 | tf_op jit(solution)/shard_map/while/body/eval_jaxpr/ppermute | solution.py:16
  149.0 18.6 %collective-permute-done = bf16[1280,2,1,128]{3,0,2,1:T(8,128)(2,1)S(1)} collective-permute-done((bf16[1280,2,1,128]{3,0,2,1:T(8,128)(2,1)S(1)}, bf16[1280,2,1,128]{3,0,2,1:T(8,128)(2,1)S(1)}, u32[]{:S(2)}, u32[]{:S(2)}) %collective-permute-start) | collective-permute-done | bytes 655392 | tf_op jit(solution)/shard_map/while/body/eval_jaxpr/ppermute | solution.py:16
  171.4 12.4 %collective-permute-done = bf16[1280,2,1,128]{3,0,2,1:T(8,128)(2,1)S(1)} collective-permute-done((bf16[1280,2,1,128]{3,0,2,1:T(8,128)(2,1)S(1)}, bf16[1280,2,1,128]{3,0,2,1:T(8,128)(2,1)S(1)}, u32[]{:S(2)}, u32[]{:S(2)}) %collective-permute-start) | collective-permute-done | bytes 655392 | tf_op jit(solution)/shard_map/while/body/eval_jaxpr/ppermute | solution.py:16
  187.5 12.4 %collective-permute-done = bf16[1280,2,1,128]{3,0,2,1:T(8,128)(2,1)S(1)} collective-permute-done((bf16[1280,2,1,128]{3,0,2,1:T(8,128)(2,1)S(1)}, bf16[1280,2,1,128]{3,0,2,1:T(8,128)(2,1)S(1)}, u32[]{:S(2)}, u32[]{:S(2)}) %collective-permute-start) | collective-permute-done | bytes 655392 | tf_op jit(solution)/shard_map/while/body/eval_jaxpr/ppermute | solution.py:16
  203.7 12.4 %collective-permute-done = bf16[1280,2,1,128]{3,0,2,1:T(8,128)(2,1)S(1)} collective-permute-done((bf16[1280,2,1,128]{3,0,2,1:T(8,128)(2,1)S(1)}, bf16[1280,2,1,128]{3,0,2,1:T(8,128)(2,1)S(1)}, u32[]{:S(2)}, u32[]{:S(2)}) %collective-permute-start) | collective-permute-done | bytes 655392 | tf_op jit(solution)/shard_map/while/body/eval_jaxpr/ppermute | solution.py:16
  219.8 12.4 %collective-permute-done = bf16[1280,2,1,128]{3,0,2,1:T(8,128)(2,1)S(1)} collective-permute-done((bf16[1280,2,1,128]{3,0,2,1:T(8,128)(2,1)S(1)}, bf16[1280,2,1,128]{3,0,2,1:T(8,128)(2,1)S(1)}, u32[]{:S(2)}, u32[]{:S(2)}) %collective-permute-start) | collective-permute-done | bytes 655392 | tf_op jit(solution)/shard_map/while/body/eval_jaxpr/ppermute | solution.py:16
  235.9 12.4 %collective-permute-done = bf16[1280,2,1,128]{3,0,2,1:T(8,128)(2,1)S(1)} collective-permute-done((bf16[1280,2,1,128]{3,0,2,1:T(8,128)(2,1)S(1)}, bf16[1280,2,1,128]{3,0,2,1:T(8,128)(2,1)S(1)}, u32[]{:S(2)}, u32[]{:S(2)}) %collective-permute-start) | collective-permute-done | bytes 655392 | tf_op jit(solution)/shard_map/while/body/eval_jaxpr/ppermute | solution.py:16
  252.1 12.4 %collective-permute-done = bf16[1280,2,1,128]{3,0,2,1:T(8,128)(2,1)S(1)} collective-permute-done((bf16[1280,2,1,128]{3,0,2,1:T(8,128)(2,1)S(1)}, bf16[1280,2,1,128]{3,0,2,1:T(8,128)(2,1)S(1)}, u32[]{:S(2)}, u32[]{:S(2)}) %collective-permute-start) | collective-permute-done | bytes 655392 | tf_op jit(solution)/shard_map/while/body/eval_jaxpr/ppermute | solution.py:16
  268.2 12.4 %collective-permute-done = bf16[1280,2,1,128]{3,0,2,1:T(8,128)(2,1)S(1)} collective-permute-done((bf16[1280,2,1,128]{3,0,2,1:T(8,128)(2,1)S(1)}, bf16[1280,2,1,128]{3,0,2,1:T(8,128)(2,1)S(1)}, u32[]{:S(2)}, u32[]{:S(2)}) %collective-permute-start) | collective-permute-done | bytes 655392 | tf_op jit(solution)/shard_map/while/body/eval_jaxpr/ppermute | solution.py:16
  286.5 117.0 %while.54 = (s32[]{:T(128)}, bf16[1024,2,1,128]{3,0,2,1:T(8,128)(2,1)S(1)}, s32[32]{0:T(128)S(1)}, s32[]{:T(128)}, bf16[4096,2,1,128]{3,1,2,0:T(2,128)(2,1)}, /*...) while((s32[]{:T(128)}, ...), condition=%wide.region_15.16_spmd, body=%wide.region_14.15_spmd.sunk | while | flops 32779 | bytes 655623 | solution.py:80
  405.6 31.8 %all-gather = f32[16,1,4,128]{3,2,1,0:T(4,128)S(1)} all-gather(f32[1,1,4,128]{3,2,1,0:T(4,128)S(1)} %fusion.71), channel_id=2, replica_groups=mesh['inst'=16,'tp'=16] {'inst'}, dimensions={0}, use_global_device_ids=true | all-gather | bytes 34816 | tf_op jit(solution)/shard_map/all_gather | solution.py:20
  437.5 22.3 %all_gather.22 = f32[16,1,1,4]{3,2,1,0:T(1,128)S(1)} all-gather(f32[1,1,1,4]{3,2,1,0:T(1,128)S(1)} %get-tuple-element.572), channel_id=1, replica_groups=mesh['inst'=16,'tp'=16] {'inst'}, dimensions={0}, use_global_device_ids=true | all-gather | bytes 272 | tf_op jit(solution)/shard_map/all_gather | solution.py:20
  459.9 19.3 %all_gather.23 = f32[16,1,1,4]{3,2,1,0:T(1,128)S(1)} all-gather(f32[1,1,1,4]{3,2,1,0:T(1,128)S(1)} %get-tuple-element.571), channel_id=1, replica_groups=mesh['inst'=16,'tp'=16] {'inst'}, dimensions={0}, use_global_device_ids=true | all-gather | bytes 272 | tf_op jit(solution)/shard_map/all_gather | solution.py:20
  479.2 7.7 %convolution_convert_fusion = bf16[256,8192]{1,0:T(8,128)(2,1)} fusion(bf16[256,512]{0,1:T(8,128)(2,1)S(1)} %bitcast.454, bf16[512,8192]{1,0:T(8,128)(2,1)} %all-gather.4.cloned.1.call-done), kind=kOutput, calls=%fused_computation.57 | convolution fusion | flops 2149580800 | bytes 12845056 | tf_op jit(solution)/shard_map/dot_general | solution.py:133
  489.5 99.4 %reduce-scatter.2.cloned.1.call-done = bf16[256,512]{1,0:T(8,128)(2,1)} async-done(((bf16[256,8192]{1,0:T(8,128)(2,1)}), bf16[256,512]{1,0:T(8,128)(2,1)}) %reduce-scatter.2.cloned.1.call-update) | async-done | bytes 262160 | tf_op jit(solution)/shard_map/reduce_scatter | solution.py:138
  (471 shorter events, 144.2 us)
Async XLA Ops:
  7.2 278.9 %copy-start = (bf16[4,128]{1,0:T(4,128)(2,1)S(1)}, bf16[4,128]{1,0:T(4,128)(2,1)}, u32[]{:S(2)}) copy-start(bf16[4,128]{1,0:T(4,128)(2,1)} %param.17) | copy-start | bytes 3076
  7.2 7.3 %copy-start.1 = (bf16[256,4,128]{2,1,0:T(4,128)(2,1)S(1)}, bf16[256,4,128]{2,1,0:T(4,128)(2,1)}, u32[]{:S(2)}) copy-start(bf16[256,4,128]{2,1,0:T(4,128)(2,1)} %param.14) | copy-start | bytes 786436
  7.2 279.3 %all-gather.6.cloned.1.call-start = ((), (), s32[]{:S(2)}) async-start(), calls=%async_computation.3 | async-start | bytes 2228224 | tf_op jit(solution)/shard_map/all_gather | solution.py:127
  7.9 471.2 %all-gather.4.cloned.1.call-start = ((), (), s32[]{:S(2)}) async-start(), calls=%async_computation.1 | async-start | bytes 8912896 | tf_op jit(solution)/shard_map/all_gather | solution.py:135
  8.7 580.3 %reduce-scatter.2.cloned.1.call-start = ((), (), s32[]{:S(2)}) async-start(), calls=%async_computation.2 | async-start | bytes 4456448 | tf_op jit(solution)/shard_map/reduce_scatter | solution.py:138
  21.6 262.8 %copy-start.2 = (s32[32,1]{0,1:T(1,128)S(1)}, s32[32,1]{0,1:T(1,128)}, u32[]{:S(2)}) copy-start(s32[32,1]{0,1:T(1,128)} %param.21) | copy-start | bytes 388
  21.6 263.0 %copy-start.3 = (s32[8]{0:T(128)S(1)}, s32[8]{0:T(128)}, u32[]{:S(2)}) copy-start(s32[8]{0:T(128)} %param.20) | copy-start | bytes 100
  21.6 264.7 %copy-start.4 = (bf16[2,1,128]{2,0,1:T(2,128)(2,1)S(1)}, bf16[2,1,128]{2,0,1:T(2,128)(2,1)}, u32[]{:S(2)}) copy-start(bf16[2,1,128]{2,0,1:T(2,128)(2,1)} %param.18) | copy-start | bytes 1540
  21.6 13.4 %collective-permute-start = (bf16[1280,2,1,128]{3,0,2,1:T(8,128)(2,1)S(1)}, bf16[1280,2,1,128]{3,0,2,1:T(8,128)(2,1)S(1)}, u32[]{:S(2)}, u32[]{:S(2)}) collective-permute-start(bf16[1280,2,1,128]{3,0,2,1:T(8,128)(2,1)S(1)} %get-tuple-element.743), channel_id=1, source_target_pairs={{240,0},{0,16},{16,32},{32,48},{48,64},{64,80},{80,96},{96,112},{1... | collective-permute-start | bytes 1966088 | tf_op jit(solution)/shard_map/while/body/eval_jaxpr/ppermute | solution.py:16
  38.7 12.5 %collective-permute-start = (bf16[1280,2,1,128]{3,0,2,1:T(8,128)(2,1)S(1)}, bf16[1280,2,1,128]{3,0,2,1:T(8,128)(2,1)S(1)}, u32[]{:S(2)}, u32[]{:S(2)}) collective-permute-start(bf16[1280,2,1,128]{3,0,2,1:T(8,128)(2,1)S(1)} %get-tuple-element.743), channel_id=1, source_target_pairs={{240,0},{0,16},{16,32},{32,48},{48,64},{64,80},{80,96},{96,112},{1... | collective-permute-start | bytes 1966088 | tf_op jit(solution)/shard_map/while/body/eval_jaxpr/ppermute | solution.py:16
  54.8 14.6 %collective-permute-start = (bf16[1280,2,1,128]{3,0,2,1:T(8,128)(2,1)S(1)}, bf16[1280,2,1,128]{3,0,2,1:T(8,128)(2,1)S(1)}, u32[]{:S(2)}, u32[]{:S(2)}) collective-permute-start(bf16[1280,2,1,128]{3,0,2,1:T(8,128)(2,1)S(1)} %get-tuple-element.743), channel_id=1, source_target_pairs={{240,0},{0,16},{16,32},{32,48},{48,64},{64,80},{80,96},{96,112},{1... | collective-permute-start | bytes 1966088 | tf_op jit(solution)/shard_map/while/body/eval_jaxpr/ppermute | solution.py:16
  73.1 12.5 %collective-permute-start = (bf16[1280,2,1,128]{3,0,2,1:T(8,128)(2,1)S(1)}, bf16[1280,2,1,128]{3,0,2,1:T(8,128)(2,1)S(1)}, u32[]{:S(2)}, u32[]{:S(2)}) collective-permute-start(bf16[1280,2,1,128]{3,0,2,1:T(8,128)(2,1)S(1)} %get-tuple-element.743), channel_id=1, source_target_pairs={{240,0},{0,16},{16,32},{32,48},{48,64},{64,80},{80,96},{96,112},{1... | collective-permute-start | bytes 1966088 | tf_op jit(solution)/shard_map/while/body/eval_jaxpr/ppermute | solution.py:16
  89.2 18.1 %collective-permute-start = (bf16[1280,2,1,128]{3,0,2,1:T(8,128)(2,1)S(1)}, bf16[1280,2,1,128]{3,0,2,1:T(8,128)(2,1)S(1)}, u32[]{:S(2)}, u32[]{:S(2)}) collective-permute-start(bf16[1280,2,1,128]{3,0,2,1:T(8,128)(2,1)S(1)} %get-tuple-element.743), channel_id=1, source_target_pairs={{240,0},{0,16},{16,32},{32,48},{48,64},{64,80},{80,96},{96,112},{1... | collective-permute-start | bytes 1966088 | tf_op jit(solution)/shard_map/while/body/eval_jaxpr/ppermute | solution.py:16
  110.9 18.1 %collective-permute-start = (bf16[1280,2,1,128]{3,0,2,1:T(8,128)(2,1)S(1)}, bf16[1280,2,1,128]{3,0,2,1:T(8,128)(2,1)S(1)}, u32[]{:S(2)}, u32[]{:S(2)}) collective-permute-start(bf16[1280,2,1,128]{3,0,2,1:T(8,128)(2,1)S(1)} %get-tuple-element.743), channel_id=1, source_target_pairs={{240,0},{0,16},{16,32},{32,48},{48,64},{64,80},{80,96},{96,112},{1... | collective-permute-start | bytes 1966088 | tf_op jit(solution)/shard_map/while/body/eval_jaxpr/ppermute | solution.py:16
  132.7 12.6 %collective-permute-start = (bf16[1280,2,1,128]{3,0,2,1:T(8,128)(2,1)S(1)}, bf16[1280,2,1,128]{3,0,2,1:T(8,128)(2,1)S(1)}, u32[]{:S(2)}, u32[]{:S(2)}) collective-permute-start(bf16[1280,2,1,128]{3,0,2,1:T(8,128)(2,1)S(1)} %get-tuple-element.743), channel_id=1, source_target_pairs={{240,0},{0,16},{16,32},{32,48},{48,64},{64,80},{80,96},{96,112},{1... | collective-permute-start | bytes 1966088 | tf_op jit(solution)/shard_map/while/body/eval_jaxpr/ppermute | solution.py:16
  148.9 18.7 %collective-permute-start = (bf16[1280,2,1,128]{3,0,2,1:T(8,128)(2,1)S(1)}, bf16[1280,2,1,128]{3,0,2,1:T(8,128)(2,1)S(1)}, u32[]{:S(2)}, u32[]{:S(2)}) collective-permute-start(bf16[1280,2,1,128]{3,0,2,1:T(8,128)(2,1)S(1)} %get-tuple-element.743), channel_id=1, source_target_pairs={{240,0},{0,16},{16,32},{32,48},{48,64},{64,80},{80,96},{96,112},{1... | collective-permute-start | bytes 1966088 | tf_op jit(solution)/shard_map/while/body/eval_jaxpr/ppermute | solution.py:16
  171.3 12.5 %collective-permute-start = (bf16[1280,2,1,128]{3,0,2,1:T(8,128)(2,1)S(1)}, bf16[1280,2,1,128]{3,0,2,1:T(8,128)(2,1)S(1)}, u32[]{:S(2)}, u32[]{:S(2)}) collective-permute-start(bf16[1280,2,1,128]{3,0,2,1:T(8,128)(2,1)S(1)} %get-tuple-element.743), channel_id=1, source_target_pairs={{240,0},{0,16},{16,32},{32,48},{48,64},{64,80},{80,96},{96,112},{1... | collective-permute-start | bytes 1966088 | tf_op jit(solution)/shard_map/while/body/eval_jaxpr/ppermute | solution.py:16
  187.4 12.5 %collective-permute-start = (bf16[1280,2,1,128]{3,0,2,1:T(8,128)(2,1)S(1)}, bf16[1280,2,1,128]{3,0,2,1:T(8,128)(2,1)S(1)}, u32[]{:S(2)}, u32[]{:S(2)}) collective-permute-start(bf16[1280,2,1,128]{3,0,2,1:T(8,128)(2,1)S(1)} %get-tuple-element.743), channel_id=1, source_target_pairs={{240,0},{0,16},{16,32},{32,48},{48,64},{64,80},{80,96},{96,112},{1... | collective-permute-start | bytes 1966088 | tf_op jit(solution)/shard_map/while/body/eval_jaxpr/ppermute | solution.py:16
  203.5 12.5 %collective-permute-start = (bf16[1280,2,1,128]{3,0,2,1:T(8,128)(2,1)S(1)}, bf16[1280,2,1,128]{3,0,2,1:T(8,128)(2,1)S(1)}, u32[]{:S(2)}, u32[]{:S(2)}) collective-permute-start(bf16[1280,2,1,128]{3,0,2,1:T(8,128)(2,1)S(1)} %get-tuple-element.743), channel_id=1, source_target_pairs={{240,0},{0,16},{16,32},{32,48},{48,64},{64,80},{80,96},{96,112},{1... | collective-permute-start | bytes 1966088 | tf_op jit(solution)/shard_map/while/body/eval_jaxpr/ppermute | solution.py:16
  219.7 12.5 %collective-permute-start = (bf16[1280,2,1,128]{3,0,2,1:T(8,128)(2,1)S(1)}, bf16[1280,2,1,128]{3,0,2,1:T(8,128)(2,1)S(1)}, u32[]{:S(2)}, u32[]{:S(2)}) collective-permute-start(bf16[1280,2,1,128]{3,0,2,1:T(8,128)(2,1)S(1)} %get-tuple-element.743), channel_id=1, source_target_pairs={{240,0},{0,16},{16,32},{32,48},{48,64},{64,80},{80,96},{96,112},{1... | collective-permute-start | bytes 1966088 | tf_op jit(solution)/shard_map/while/body/eval_jaxpr/ppermute | solution.py:16
  235.8 12.5 %collective-permute-start = (bf16[1280,2,1,128]{3,0,2,1:T(8,128)(2,1)S(1)}, bf16[1280,2,1,128]{3,0,2,1:T(8,128)(2,1)S(1)}, u32[]{:S(2)}, u32[]{:S(2)}) collective-permute-start(bf16[1280,2,1,128]{3,0,2,1:T(8,128)(2,1)S(1)} %get-tuple-element.743), channel_id=1, source_target_pairs={{240,0},{0,16},{16,32},{32,48},{48,64},{64,80},{80,96},{96,112},{1... | collective-permute-start | bytes 1966088 | tf_op jit(solution)/shard_map/while/body/eval_jaxpr/ppermute | solution.py:16
  251.9 12.5 %collective-permute-start = (bf16[1280,2,1,128]{3,0,2,1:T(8,128)(2,1)S(1)}, bf16[1280,2,1,128]{3,0,2,1:T(8,128)(2,1)S(1)}, u32[]{:S(2)}, u32[]{:S(2)}) collective-permute-start(bf16[1280,2,1,128]{3,0,2,1:T(8,128)(2,1)S(1)} %get-tuple-element.743), channel_id=1, source_target_pairs={{240,0},{0,16},{16,32},{32,48},{48,64},{64,80},{80,96},{96,112},{1... | collective-permute-start | bytes 1966088 | tf_op jit(solution)/shard_map/while/body/eval_jaxpr/ppermute | solution.py:16
  268.1 12.5 %collective-permute-start = (bf16[1280,2,1,128]{3,0,2,1:T(8,128)(2,1)S(1)}, bf16[1280,2,1,128]{3,0,2,1:T(8,128)(2,1)S(1)}, u32[]{:S(2)}, u32[]{:S(2)}) collective-permute-start(bf16[1280,2,1,128]{3,0,2,1:T(8,128)(2,1)S(1)} %get-tuple-element.743), channel_id=1, source_target_pairs={{240,0},{0,16},{16,32},{32,48},{48,64},{64,80},{80,96},{96,112},{1... | collective-permute-start | bytes 1966088 | tf_op jit(solution)/shard_map/while/body/eval_jaxpr/ppermute | solution.py:16
Sparse Core Ops, SparseCore 0:
  10.7 58.5 all-gather.5
  71.8 99.9 all-gather.3
  487.0 101.8 reduce-scatter.1
where the time goes:
time: 598 us; the launch traced here: 595 us
  waiting for transfers between devices  307 us (51%)
  blocking collectives  73.4 us (12%)
  local copies, waits for them, and re-layouts  71.9 us (12%)
  matrix products  56.1 us (9%)
  loops' own time  44.8 us (7%)
  other arithmetic  26.3 us (4%)
  between operations  14.6 us (2%)
    ppermute x15, waiting for transfers between devices, from_behind(): return lax.ppermute(block, axis, route)  206 us
    reduce_scatter x1, waiting for transfers between devices, on_device(): lax.psum_scatter(terms.astype(jnp.bfloat16), 'tp', scatter_dimension=1, t...  99.4 us
    all_gather x3, blocking collectives, combined_all(): everything = jax.tree.map(lambda part: lax.all_gather(part, axis), value)  73.4 us
    another operation x1, loops' own time, place_blocks(): return lax.fori_loop(0, count, put, cache)  43.4 us
    dynamic_slice x32, local copies, waits for them, and re-layouts, put(): incoming = lax.dynamic_slice_in_dim(rows_in, index * BLK, BLK, 0)  28.5 us
    dot_general x34, matrix products, attend(): jnp.einsum('rkgn,nkd->rkgd', weights.astype(jnp.bfloat16), key_value[:, 1...  28.1 us
    dot_general x34, matrix products, attend(): jnp.einsum('rkgd,nkd->rkgn', queries, key_value[:, 0], preferred_element_...  20.2 us
    dynamic_slice x32, local copies, waits for them, and re-layouts, put(): destination_members[index] == own_index  18.8 us
  transfers between devices with their start and end apart: 18, of which 16 were waited for; matrix products, arithmetic and copies ran while one was open for 25% of the time, Pallas kernels for 0%

commit v1 on v0

v1 whole, which is shorter than its diff:
```python
import functools
import jax
import jax.numpy as jnp
from jax import lax
from jax.experimental import pallas as pl
from jax.experimental.pallas import tpu as pltpu
from jax.sharding import PartitionSpec as P

BLK = 128
CAP = 8
ROWS = 256
HEADS = 4
HD = 128
Q = ROWS * HEADS
KEYS = 1280
PIECE = 256
NX = 4
NS = 4
NZ = 8
NEG = -1e30
C2 = float(HD ** -0.5 * 1.4426950408889634)
MESH = pl.DeviceIdType.MESH


def signal(where):
    pl.semaphore_signal(
        pltpu.get_barrier_semaphore(), inc=1, device_id=where, device_id_type=MESH
    )


def attention_kernel(
    q_hbm, k_hbm, vt_hbm, probe_ref, pair_ref,
    a_ref, dec_ref,
    qbuf, kbuf, vbuf, acc, m_s, l_s, s_buf,
    o_send, o_recv, st_send, st_recv, qd, d_all,
    loc_sem, q_ss, q_rs, k_ss, k_rs, v_ss, v_rs, o_ss, o_rs, t_ss, t_rs, d_ss, d_rs,
):
    me = lax.axis_index("inst")
    x, s = me // NS, me % NS
    s1 = s + 1 - 2 * (s % 2)
    s2 = (s + 2) % NS
    s3 = (s1 + 2) % NS

    def at_x(d):
        return {"inst": ((x + d) % NX) * NS + s}

    def at_s(t):
        return {"inst": x * NS + t}

    def remote(src, dst, ss, rs, where):
        return pltpu.make_async_remote_copy(
            src_ref=src, dst_ref=dst, send_sem=ss, recv_sem=rs,
            device_id=where, device_id_type=MESH,
        )

    own = [
        pltpu.make_async_copy(k_hbm, kbuf.at[s], loc_sem.at[0]),
        pltpu.make_async_copy(q_hbm, qbuf.at[0], loc_sem.at[1]),
        pltpu.make_async_copy(vt_hbm, vbuf.at[s], loc_sem.at[2]),
    ]
    for copy in own:
        copy.start()

    for d in (1, 2, 3):
        signal(at_x(d))
    signal(at_s(s1))
    signal(at_s(s2))
    pl.semaphore_wait(pltpu.get_barrier_semaphore(), 5)

    def q_push(d):
        return remote(q_hbm, qbuf.at[NX - d], q_ss.at[d - 1], q_rs.at[NX - d - 1], at_x(d))

    k_push = [
        remote(k_hbm, kbuf.at[s], k_ss.at[0], k_rs.at[0], at_s(s1)),
        remote(k_hbm, kbuf.at[s], k_ss.at[1], k_rs.at[1], at_s(s2)),
        remote(kbuf.at[s2], kbuf.at[s2], k_ss.at[2], k_rs.at[2], at_s(s1)),
    ]
    v_push = [
        remote(vt_hbm, vbuf.at[s], v_ss.at[0], v_rs.at[0], at_s(s1)),
        remote(vt_hbm, vbuf.at[s], v_ss.at[1], v_rs.at[1], at_s(s2)),
        remote(vbuf.at[s2], vbuf.at[s2], v_ss.at[2], v_rs.at[2], at_s(s1)),
    ]
    k_push[0].start()
    q_push(1).start()
    q_push(3).start()
    v_push[0].start()
    k_push[1].start()
    v_push[1].start()

    qd[...] = jnp.zeros_like(qd)
    qd[0:HEADS, :] = probe_ref[...]
    acc[...] = jnp.zeros_like(acc)
    l_s[...] = jnp.zeros_like(l_s)
    m_s[...] = jnp.full(m_s.shape, NEG, jnp.float32)

    key_of = lax.broadcasted_iota(jnp.int32, (PIECE, Q), 0)
    row_of = lax.broadcasted_iota(jnp.int32, (PIECE, Q), 1) % ROWS

    def scores(buf, q, k, j, highest):
        part = lax.dot_general(
            kbuf[k, j * PIECE:(j + 1) * PIECE, :], qbuf[q],
            (((1,), (1,)), ((), ())), preferred_element_type=jnp.float32,
        )
        if j == KEYS // PIECE - 1:
            ahead = ROWS * (((x + q) % NX) * NS + s - (x * NS + k))
            part = jnp.where(key_of - row_of <= ahead, part, NEG)
        s_buf[buf, j * PIECE:(j + 1) * PIECE, :] = part
        return jnp.maximum(highest, jnp.max(part.reshape(PIECE // 8, 8, Q), axis=0))

    lowest = jnp.full((8, Q), NEG, jnp.float32)

    def unit(buf, q, k, highest, following):
        m_old = m_s[q]
        m_new = jnp.maximum(
            m_old, jnp.broadcast_to(jnp.max(highest, axis=0, keepdims=True), (8, Q))
        )
        m_s[q] = m_new
        alpha = jnp.exp2((m_old - m_new) * C2)
        top = m_new[0:1]
        total = acc[q] * alpha[0:1]
        norm = l_s[q] * alpha
        after = lowest
        for j in range(KEYS // PIECE):
            if following is not None:
                after = scores(1 - buf, following[0], following[1], j, after)
            p = jnp.exp2((s_buf[buf, j * PIECE:(j + 1) * PIECE, :] - top) * C2)
            norm = norm + jnp.sum(p.reshape(PIECE // 8, 8, Q), axis=0)
            total = total + jnp.dot(
                vbuf[k, :, j * PIECE:(j + 1) * PIECE], p.astype(jnp.bfloat16),
                preferred_element_type=jnp.float32,
            )
        acc[q] = total
        l_s[q] = norm
        return after

    def q_at(i):
        phase, n = i // 4, i % 4
        near = n + n // 2 - 2 * (n // 3)
        far = 2 - n + 3 * (n // 2) - 2 * (n // 3)
        return near * (1 - phase) + far * phase

    def k_at(i):
        phase = i // 4
        return s * (1 - phase) + s2 * phase, s1 * (1 - phase) + s3 * phase

    def normalised(q, t):
        cols = slice(t * 128, (t + 1) * 128)
        norm = jnp.sum(l_s[q, :, cols], axis=0, keepdims=True)
        return acc[q, :, cols] / norm, m_s[q, 0:1, cols] * C2 + jnp.log2(norm)

    def o_push(d):
        return remote(
            o_send.at[d - 1], o_recv.at[NX - d - 1], o_ss.at[d - 1], o_rs.at[NX - d - 1], at_x(d)
        )

    def t_push(d):
        return remote(
            st_send.at[d - 1], st_recv.at[NX - d - 1], t_ss.at[d - 1], t_rs.at[NX - d - 1], at_x(d)
        )

    for copy in own:
        copy.wait()
    highest = lowest
    for j in range(KEYS // PIECE):
        highest = scores(0, 0, s, j, highest)

    def pair(i, highest):
        q = q_at(i)
        ka, kb = k_at(i)

        @pl.when(i == 0)
        def _():
            k_push[0].wait_recv()
            v_push[0].wait_recv()

        @pl.when(i == 4)
        def _():
            k_push[2].wait_recv()
            v_push[2].wait_recv()

        highest = unit(0, q, ka, highest, (q, kb))

        @pl.when(i == 0)
        def _():
            q_push(1).wait_send()
            q_push(2).start()
            q_push(3).wait_recv()

        @pl.when(i == 1)
        def _():
            q_push(1).wait_recv()

        @pl.when(i == 2)
        def _():
            q_push(2).wait_recv()

        @pl.when(i == 3)
        def _():
            k_push[1].wait_recv()
            k_push[2].start()
            v_push[1].wait_recv()
            v_push[2].start()

        highest = unit(1, q, kb, highest, (q_at(i + 1), k_at(i + 1)[0]))

        @pl.when(i >= 4)
        def _():
            for t in range(Q // 128):
                o, lse = normalised(q, t)
                o_send[q - 1, :, t * 128:(t + 1) * 128] = o.astype(jnp.bfloat16)
                st_send[q - 1, t:t + 1, :] = lse
            o_push(q).start()
            t_push(q).start()

        return highest

    highest = lax.fori_loop(0, 7, pair, highest)
    highest = unit(0, 0, s2, highest, (0, s3))
    unit(1, 0, s3, highest, None)

    dm = jnp.full((1, 128), NEG, jnp.float32)
    dl = jnp.zeros((1, 128), jnp.float32)
    da = jnp.zeros((HD, 128), jnp.float32)
    for k in range(NS):
        part = lax.dot_general(
            kbuf[k], qd[...], (((1,), (1,)), ((), ())), preferred_element_type=jnp.float32
        )
        new = jnp.maximum(dm, jnp.max(part, axis=0, keepdims=True))
        alpha = jnp.exp2((dm - new) * C2)
        p = jnp.exp2((part - new) * C2)
        dl = dl * alpha + jnp.sum(p, axis=0, keepdims=True)
        da = da * alpha + jnp.dot(
            vbuf[k], p.astype(jnp.bfloat16), preferred_element_type=jnp.float32
        )
        dm = new
    d_all[x, 0:8, :] = jnp.transpose(da)[0:8]
    d_all[x, 8:16, :] = jnp.transpose(jnp.broadcast_to(dm, (128, 128)))[0:8]
    d_all[x, 16:24, :] = jnp.transpose(jnp.broadcast_to(dl, (128, 128)))[0:8]

    def d_push(d):
        return remote(d_all.at[x], d_all.at[x], d_ss.at[d - 1], d_rs.at[NX - d - 1], at_x(d))

    for d in (1, 2, 3):
        d_push(d).start()

    for d in (1, 2, 3):
        o_push(d).wait_recv()
        t_push(d).wait_recv()
    for t in range(Q // 128):
        cols = slice(t * 128, (t + 1) * 128)
        o, lse = normalised(0, t)
        rest = [st_recv[d, t:t + 1, :] for d in range(3)]
        top = functools.reduce(jnp.maximum, rest, lse)
        weight = jnp.exp2(lse - top)
        total, norm = o * weight, weight
        for d in range(3):
            weight = jnp.exp2(rest[d] - top)
            total = total + o_recv[d, :, cols].astype(jnp.float32) * weight
            norm = norm + weight
        h, r = t // 2, (t % 2) * 128
        a_ref[r:r + 128, h * HD:(h + 1) * HD] = jnp.transpose(total / norm).astype(jnp.bfloat16)

    for d in (1, 2, 3):
        d_push(d).wait_recv()
    query = qd[0:8, :].astype(jnp.float32)
    last = jnp.sum(query * pair_ref[0:1, :].astype(jnp.float32), axis=1, keepdims=True)
    last = jnp.broadcast_to(last, (8, HD))
    top = last
    for d in range(NX):
        top = jnp.maximum(top, d_all[d, 8:16, :])
    weight = jnp.exp2((last - top) * C2)
    total, norm = weight * pair_ref[1:2, :].astype(jnp.float32), weight
    for d in range(NX):
        weight = jnp.exp2((d_all[d, 8:16, :] - top) * C2)
        total = total + d_all[d, 0:8, :] * weight
        norm = norm + d_all[d, 16:24, :] * weight
    dec_ref[...] = (total / norm)[0:HEADS].astype(jnp.bfloat16)

    for d in (1, 2, 3):
        o_push(d).wait_send()
        t_push(d).wait_send()
        d_push(d).wait_send()
    q_push(2).wait_send()
    q_push(3).wait_send()
    for copy in k_push + v_push:
        copy.wait_send()


def attention(q, k, vt, probe, pair):
    dma = pltpu.SemaphoreType.DMA
    return pl.pallas_call(
        attention_kernel,
        out_shape=(
            jax.ShapeDtypeStruct((ROWS, HEADS * HD), jnp.bfloat16),
            jax.ShapeDtypeStruct((HEADS, HD), jnp.bfloat16),
        ),
        in_specs=[pl.BlockSpec(memory_space=pl.ANY)] * 3
        + [pl.BlockSpec(memory_space=pltpu.VMEM)] * 2,
        out_specs=(pl.BlockSpec(memory_space=pltpu.VMEM),) * 2,
        scratch_shapes=[
            pltpu.VMEM((NX, Q, HD), jnp.bfloat16),
            pltpu.VMEM((NS, KEYS, HD), jnp.bfloat16),
            pltpu.VMEM((NS, HD, KEYS), jnp.bfloat16),
            pltpu.VMEM((NX, HD, Q), jnp.float32),
            pltpu.VMEM((NX, 8, Q), jnp.float32),
            pltpu.VMEM((NX, 8, Q), jnp.float32),
            pltpu.VMEM((2, KEYS, Q), jnp.float32),
            pltpu.VMEM((3, HD, Q), jnp.bfloat16),
            pltpu.VMEM((3, HD, Q), jnp.bfloat16),
            pltpu.VMEM((3, Q // 128, 128), jnp.float32),
            pltpu.VMEM((3, Q // 128, 128), jnp.float32),
            pltpu.VMEM((128, HD), jnp.bfloat16),
            pltpu.VMEM((NX, 24, 128), jnp.float32),
        ] + [dma((3,))] * 13,
        compiler_params=pltpu.CompilerParams(
            collective_id=0, has_side_effects=True, vmem_limit_bytes=60 * 2 ** 20
        ),
        cost_estimate=pl.CostEstimate(
            flops=4 * NX * Q * NS * KEYS * HD, bytes_accessed=4 * 2 ** 20,
            transcendentals=NX * Q * NS * KEYS,
        ),
        name="attention",
    )(q, k, vt, probe, pair)


def projection_kernel(
    a_hbm, w_hbm, y_ref,
    abuf, wbuf, sbuf, rbuf, a_sem, w_sem, a_ss, a_rs, ss, rs,
):
    tp = lax.axis_index("tp")
    z, half = tp // 2, tp % 2

    def at_z(d):
        return {"tp": ((z + d + NZ) % NZ) * 2 + half}

    partner = {"tp": z * 2 + 1 - half}
    order = [4, 3, -3, 2, -2, 1, -1, 0]

    own = pltpu.make_async_copy(a_hbm, abuf.at[half], a_sem)
    own.start()
    blocks = {}
    for n, d in enumerate(order):
        chunk = (z + d + NZ) % NZ
        blocks[d] = pltpu.make_async_copy(w_hbm.at[chunk], wbuf.at[n], w_sem.at[n])
        blocks[d].start()

    signal(partner)
    signal(at_z(1))
    signal(at_z(-1))
    pl.semaphore_wait(pltpu.get_barrier_semaphore(), 3)

    swap = pltpu.make_async_remote_copy(
        src_ref=a_hbm, dst_ref=abuf.at[half], send_sem=a_ss, recv_sem=a_rs,
        device_id=partner, device_id_type=MESH,
    )
    swap.start()
    own.wait()
    swap.wait_recv()

    def term(d):
        n = order.index(d)
        blocks[d].wait()
        return jnp.dot(
            abuf[0], wbuf[n, 0:512, :], preferred_element_type=jnp.float32
        ) + jnp.dot(abuf[1], wbuf[n, 512:1024, :], preferred_element_type=jnp.float32)

    def push(way, step, part):
        n = (way * 4 + step) * 2 + part
        return pltpu.make_async_remote_copy(
            src_ref=sbuf.at[n], dst_ref=rbuf.at[n], send_sem=ss.at[n], recv_sem=rs.at[n],
            device_id=at_z(1 if way == 0 else -1), device_id_type=MESH,
        )

    sent = []

    def send(way, step, part, value):
        sbuf[(way * 4 + step) * 2 + part] = value.astype(jnp.bfloat16)
        copy = push(way, step, part)
        copy.start()
        sent.append(copy)

    def arrived(way, step, part):
        push(way, step, part).wait_recv()
        return rbuf[(way * 4 + step) * 2 + part].astype(jnp.float32)

    def rows(value, part):
        return value[part * 128:(part + 1) * 128]

    y = term(4)
    send(0, 0, 0, rows(y, 0))
    send(1, 0, 1, rows(y, 1))
    right, left = term(3), term(-3)
    send(0, 1, 1, rows(right, 1))
    send(1, 1, 0, rows(left, 0))
    send(0, 1, 0, rows(right, 0) + arrived(0, 0, 0))
    send(1, 1, 1, rows(left, 1) + arrived(1, 0, 1))
    for step in (2, 3):
        right, left = term(4 - step), term(step - 4)
        for first in (0, 1):
            send(0, step, 1 - first, rows(right, 1 - first) + arrived(0, step - 1, 1 - first))
            send(1, step, first, rows(left, first) + arrived(1, step - 1, first))
    y = term(0)
    for part in (1, 0):
        total = rows(y, part) + arrived(0, 3, part) + arrived(1, 3, part)
        y_ref[part * 128:(part + 1) * 128, :] = total.astype(jnp.bfloat16)
    swap.wait_send()
    for copy in sent:
        copy.wait_send()


def projection(a, w):
    dma = pltpu.SemaphoreType.DMA
    return pl.pallas_call(
        projection_kernel,
        out_shape=jax.ShapeDtypeStruct((ROWS, 512), jnp.bfloat16),
        in_specs=[pl.BlockSpec(memory_space=pl.ANY)] * 2,
        out_specs=pl.BlockSpec(memory_space=pltpu.VMEM),
        scratch_shapes=[
            pltpu.VMEM((2, ROWS, 512), jnp.bfloat16),
            pltpu.VMEM((NZ, 1024, 512), jnp.bfloat16),
            pltpu.VMEM((16, 128, 512), jnp.bfloat16),
            pltpu.VMEM((16, 128, 512), jnp.bfloat16),
            dma, dma((NZ,)), dma, dma, dma((16,)), dma((16,)),
        ],
        compiler_params=pltpu.CompilerParams(
            collective_id=1, has_side_effects=True, vmem_limit_bytes=60 * 2 ** 20
        ),
        cost_estimate=pl.CostEstimate(
            flops=2 * ROWS * 1024 * 4096, bytes_accessed=9 * 2 ** 20, transcendentals=0
        ),
        name="projection",
    )(a, w)


def placement_kernel(ids_ref, member_ref, rows_hbm, out_hbm, zeros, sem):
    me = lax.axis_index("inst")
    size = BLK * 2
    zeros[...] = jnp.zeros_like(zeros)

    def take(b, taken):
        mine = ids_ref[member_ref[b]] == me

        @pl.when(mine)
        def _():
            pltpu.make_async_copy(
                rows_hbm.at[pl.ds(b * size, size)], out_hbm.at[pl.ds(taken * size, size)], sem
            ).start()

        return taken + mine.astype(jnp.int32)

    taken = lax.fori_loop(0, 32, take, 0)

    def clear(n, carry):
        pltpu.make_async_copy(zeros, out_hbm.at[pl.ds(n * size, size)], sem).start()
        return carry

    lax.fori_loop(taken, CAP, clear, 0)
    pltpu.make_async_copy(rows_hbm.at[pl.ds(0, CAP * size)], out_hbm, sem).wait()


def placement(ids, members, rows):
    return pl.pallas_call(
        placement_kernel,
        out_shape=jax.ShapeDtypeStruct((CAP * BLK * 2, HD), jnp.bfloat16),
        in_specs=[pl.BlockSpec(memory_space=pltpu.SMEM)] * 2
        + [pl.BlockSpec(memory_space=pl.ANY)],
        out_specs=pl.BlockSpec(memory_space=pl.ANY),
        scratch_shapes=[pltpu.VMEM((BLK * 2, HD), jnp.bfloat16), pltpu.SemaphoreType.DMA],
        compiler_params=pltpu.CompilerParams(vmem_limit_bytes=60 * 2 ** 20),
        name="placement",
    )(ids, members, rows)


def on_device(
    fresh_segment_probes,
    fresh_segment_pairs,
    earlier_stored_pairs,
    emitted_token_probe,
    emitted_token_pair,
    final_projection_weights,
    remaining_instance_ids,
    segment_destination_member,
):
    route = []
    inst_size, tp_size = lax.axis_size("inst"), lax.axis_size("tp")
    for i in range(inst_size):
        for t in range(tp_size):
            core, low = i % 2, t % 2
            route.append((i * tp_size + t, (i - core + low) * tp_size + t - low + core))
    swapped = lax.ppermute(final_projection_weights, ("inst", "tp"), route)
    weights = lax.all_gather(swapped, "inst", axis=0).reshape(NZ, 1024, 512)
    fresh = fresh_segment_pairs.reshape(ROWS * 2, HD)
    moved = lax.all_gather(fresh, "inst", axis=0, tiled=True)

    q = jnp.transpose(fresh_segment_probes, (1, 0, 2)).reshape(Q, HD)
    pairs = jnp.concatenate([earlier_stored_pairs, fresh_segment_pairs], axis=0)[:, :, 0, :]
    a, decode_attention = attention(
        q, pairs[:, 0], pairs[:, 1].T, emitted_token_probe, emitted_token_pair.reshape(2, HD)
    )
    cache = placement(
        remaining_instance_ids, segment_destination_member.reshape(-1), moved
    ).reshape(1, CAP * BLK, 2, 1, HD)
    span_hidden = projection(a, weights)
    return span_hidden, cache, decode_attention


def solution(mesh):
    return jax.shard_map(
        on_device,
        mesh=mesh,
        in_specs=(
            P("inst", "tp", None),
            P("inst", None, "tp", None),
            P("inst", None, "tp", None),
            P("tp", None),
            P(None, "tp", None),
            P("tp", "inst"),
            P(),
            P(),
        ),
        out_specs=(P("inst", "tp"), P("inst", None, None, "tp", None), P("tp", None)),
        check_vma=False,
    )
```

time: 598 us -> 196 us (0.33)
  waiting for transfers between devices: 307 us -> 76.9 us
  Pallas kernels: 0 us -> 93.9 us
  blocking collectives: 73.4 us -> 0 us
  local copies, waits for them, and re-layouts: 71.9 us -> 7.77 us
  matrix products: 56.1 us -> 0 us
  loops' own time: 44.8 us -> 0 us
  other arithmetic: 26.3 us -> 0.04 us
    ppermute x15 -> x1, waiting for transfers between devices: 206 us -> 0.01 us  [on_device(): swapped = lax.ppermute(final_projection_weights, ('inst', 'tp'), route)]
    reduce_scatter x1 -> x0, waiting for transfers between devices: 99.4 us -> none  [on_device(): lax.psum_scatter(terms.astype(jnp.bfloat16), 'tp', scatter_dimension=1, t...]
    pallas_call x0 -> x3, Pallas kernels: none -> 93.9 us  [the longest x1 54.3 us: attention(): pl.pallas_call(attention_kernel, out_shape=(jax.ShapeDtypeStruct((ROWS, H...]
    all_gather x2, waiting for transfers between devices: 0.02 us -> 76.2 us  [the longest x1 74.9 us: on_device(): weights = lax.all_gather(swapped, 'inst', axis=0).reshape(NZ, 1024, 512)]
    all_gather x3 -> x0, blocking collectives: 73.4 us -> none  [combined_all(): everything = jax.tree.map(lambda part: lax.all_gather(part, axis), value)]
    dynamic_slice x128 -> x0, local copies, waits for them, and re-layouts: 66.6 us -> none  [the longest x32 28.5 us: put(): incoming = lax.dynamic_slice_in_dim(rows_in, index * BLK, BLK, 0)]
    dot_general x70 -> x0, matrix products: 56.1 us -> none  [the longest x34 28.1 us: attend(): jnp.einsum('rkgn,nkd->rkgd', weights.astype(jnp.bfloat16), key_value[:, 1...]
    another operation x3 -> x0, loops' own time: 44.8 us -> none  [the longest x1 43.4 us: place_blocks(): return lax.fori_loop(0, count, put, cache)]
  transfers between devices with their start and end apart: 18 -> 3, of which waited for: 16 -> 2; matrix products, arithmetic and copies ran while one was open for 25% -> 2% of each run, Pallas kernels for 0% -> 31%
where the time goes in v1:
time: 196 us; the launch traced here: 195 us
  Pallas kernels  93.9 us (48%)
  waiting for transfers between devices  76.9 us (39%)
  between operations  14.1 us (7%)
  local copies, waits for them, and re-layouts  7.77 us (4%)
    all_gather x1, waiting for transfers between devices, on_device(): weights = lax.all_gather(swapped, 'inst', axis=0).reshape(NZ, 1024, 512)  74.9 us
    pallas_call x1, Pallas kernels, attention(): pl.pallas_call(attention_kernel, out_shape=(jax.ShapeDtypeStruct((ROWS, H...  54.3 us
    pallas_call x1, Pallas kernels, projection(): pl.pallas_call(projection_kernel, out_shape=jax.ShapeDtypeStruct((ROWS, 5...  33.9 us
    pallas_call x1, Pallas kernels, placement(): pl.pallas_call(placement_kernel, out_shape=jax.ShapeDtypeStruct((CAP * BL...  5.79 us
    unnamed x10, local copies, waits for them, and re-layouts  5.37 us
  transfers between devices with their start and end apart: 3, of which 2 were waited for; matrix products, arithmetic and copies ran while one was open for 2% of the time, Pallas kernels for 31%

profile of v1, /device:TPU:2, one launch (start us, length us, event | category | flops | bytes accessed | tf_op | source)
XLA Modules:
  0.0 194.6 jit_solution(2499544635324991807)
XLA Ops:
  7.2 0.0 all-gather.4.cloned.1.call-start
  7.2 0.7 all-gather.4.cloned.1.call-update
  7.9 0.0 all-gather.6.cloned.1.call-start
  7.9 1.7 collective-permute-start
  9.6 0.0 collective-permute-done
  9.6 0.0 copy-start
  9.6 0.8 copy-done
  10.5 0.0 all-gather.6.cloned.1.call-update
  10.5 1.0 copy.13
  11.5 1.3 copy.12
  12.9 0.0 copy-start.1
  12.9 0.8 slice_bitcast_fusion
  13.7 0.9 copy.14.k_hbm
  14.5 0.0 copy-done.1
  14.5 0.7 copy.11
  15.3 54.3 %attention.1 = (bf16[256,512]{1,0:T(8,128)(2,1)}, bf16[4,128]{1,0:T(4,128)(2,1)}) custom-call(bf16[1024,128]{1,0:T(8,128)(2,1)} %bitcast.21, bf16[1280,128]{1,0:T(8,128)(2,1)} %copy.14.k_hbm, bf16[128,1280]{1,0:T(8,128)(2,1)} %get-tuple-element.10.vt_hbm, bf16[4,128]{1,0:T(4,128)(2,1)} %probe_ref.1, bf16[2,128]{1,0:T(2,128)(2,1)} %bitcast.23), custom_call_target="tpu_custom_call" | custom-call | flops 10737418240 | bytes 4194304 | tf_op jit(solution)/shard_map/attention/pallas_call | solution.py:291
  69.6 1.3 all-gather.4.cloned.1.call-done.rows_hbm
  70.9 5.8 %placement.1 = bf16[2048,128]{1,0:T(8,128)(2,1)} custom-call(s32[8]{0:T(128)} %ids_ref.1, s32[32]{0:T(128)} %bitcast.22, bf16[8192,128]{1,0:T(8,128)(2,1)} %all-gather.4.cloned.1.call-done.rows_hbm), custom_call_target="tpu_custom_call" | custom-call | tf_op jit(solution)/shard_map/placement/pallas_call | solution.py:462
  76.7 74.9 %all-gather.6.cloned.1.call-done = bf16[8192,512]{1,0:T(8,128)(2,1)} async-done(((bf16[512,512]{1,0:T(8,128)(2,1)}), bf16[8192,512]{1,0:T(8,128)(2,1)}) %all-gather.6.cloned.1.call-update) | async-done | bytes 8388624 | tf_op jit(solution)/shard_map/all_gather | solution.py:491
  151.6 0.0 copy-start.2
  151.6 33.9 %projection.1 = bf16[256,512]{1,0:T(8,128)(2,1)} custom-call(bf16[256,512]{1,0:T(8,128)(2,1)} %get-tuple-element.5.a_hbm, bf16[8,1024,512]{2,1,0:T(8,128)(2,1)} %bitcast.17), custom_call_target="tpu_custom_call" | custom-call | flops 2147483648 | bytes 9437184 | tf_op jit(solution)/shard_map/projection/pallas_call | solution.py:413
  185.5 1.7 copy.18
  187.2 0.0 copy-done.2
  187.2 0.6 copy.19
  (1 shorter events, 0.0 us)
Async XLA Ops:
  7.2 63.7 %all-gather.4.cloned.1.call-start = ((), (), s32[]{:S(2)}) async-start(), calls=%async_computation | async-start | bytes 2228224 | tf_op jit(solution)/shard_map/all_gather | solution.py:493
  7.9 143.7 %all-gather.6.cloned.1.call-start = ((), (), s32[]{:S(2)}) async-start(), calls=%async_computation.1 | async-start | bytes 8912896 | tf_op jit(solution)/shard_map/all_gather | solution.py:491
  7.9 1.7 collective-permute-start
  9.6 0.8 copy-start
  12.9 1.7 copy-start.1
  151.6 35.6 %copy-start.2 = (bf16[4,128]{1,0:T(4,128)(2,1)S(1)}, bf16[4,128]{1,0:T(4,128)(2,1)}, u32[]{:S(2)}) copy-start(bf16[4,128]{1,0:T(4,128)(2,1)} %get-tuple-element.17) | copy-start | bytes 3076
Sparse Core Ops, SparseCore 0:
  10.7 60.1 all-gather.3
  73.6 77.9 all-gather.5

commit v2 on v1

--- a/solution.py
+++ b/solution.py
@@ -28,16 +28,20 @@
     )
 
 
-def attention_kernel(
-    q_hbm, k_hbm, vt_hbm, probe_ref, pair_ref,
-    a_ref, dec_ref,
-    qbuf, kbuf, vbuf, acc, m_s, l_s, s_buf,
-    o_send, o_recv, st_send, st_recv, qd, d_all,
+def fused_kernel(
+    q_hbm, fresh_hbm, prefix_hbm, probe_ref, pair_ref, w_hbm,
+    y_ref, dec_ref,
+    raw, raw_q, stage, qbuf, kbuf, vbuf, acc, m_s, l_s, s_buf,
+    o_send, o_recv, st_send, st_recv, qd, d_all, w_all, abuf, sbuf, rbuf,
     loc_sem, q_ss, q_rs, k_ss, k_rs, v_ss, v_rs, o_ss, o_rs, t_ss, t_rs, d_ss, d_rs,
+    wy_ss, wy_rs, wx_ss, wx_rs, wf_ss, wf_rs, wc_ss, wc_rs, a_ss, a_rs, r_ss, r_rs,
 ):
     me = lax.axis_index("inst")
+    tp = lax.axis_index("tp")
     x, s = me // NS, me % NS
-    s1 = s + 1 - 2 * (s % 2)
+    far, core = s // 2, s % 2
+    z, low = tp // 2, tp % 2
+    s1 = s + 1 - 2 * core
     s2 = (s + 2) % NS
     s3 = (s1 + 2) % NS
 
@@ -46,6 +50,15 @@
 
     def at_s(t):
         return {"inst": x * NS + t}
+
+    def at_w(t):
+        return {"inst": x * NS + 2 * t + low, "tp": z * 2 + core}
+
+    def at_z(d, t):
+        return {"inst": x * NS + t, "tp": ((z + d + NZ) % NZ) * 2 + low}
+
+    def at_low(t):
+        return {"inst": x * NS + t, "tp": z * 2 + 1 - low}
 
     def remote(src, dst, ss, rs, where):
         return pltpu.make_async_remote_copy(
@@ -53,39 +66,117 @@
             device_id=where, device_id_type=MESH,
         )
 
-    own = [
-        pltpu.make_async_copy(k_hbm, kbuf.at[s], loc_sem.at[0]),
-        pltpu.make_async_copy(q_hbm, qbuf.at[0], loc_sem.at[1]),
-        pltpu.make_async_copy(vt_hbm, vbuf.at[s], loc_sem.at[2]),
+    load = [
+        pltpu.make_async_copy(prefix_hbm, raw.at[0:2048], loc_sem.at[0]),
+        pltpu.make_async_copy(fresh_hbm, raw.at[2048:2560], loc_sem.at[1]),
+        pltpu.make_async_copy(q_hbm, raw_q, loc_sem.at[2]),
     ]
-    for copy in own:
+    for copy in load:
         copy.start()
 
     for d in (1, 2, 3):
         signal(at_x(d))
     signal(at_s(s1))
     signal(at_s(s2))
-    pl.semaphore_wait(pltpu.get_barrier_semaphore(), 5)
+    signal(at_low(s))
+    signal(at_low(s2))
+    for d in (1, -1):
+        signal(at_z(d, s))
+        signal(at_z(d, s2))
+
+    @pl.when(core != low)
+    def _():
+        signal(at_w(0))
+        signal(at_w(1))
+
+    load[0].wait()
+    load[1].wait()
+    stage[...] = raw[...].astype(jnp.float32)
+    kbuf[s] = stage[pl.ds(0, KEYS, stride=2), :].astype(jnp.bfloat16)
+    load[2].wait()
+    vbuf[s] = jnp.transpose(stage[pl.ds(1, KEYS, stride=2), :]).astype(jnp.bfloat16)
+    stage[0:Q] = raw_q[...].astype(jnp.float32)
+    for h in range(HEADS):
+        qbuf[0, h * ROWS:(h + 1) * ROWS, :] = stage[
+            pl.ds(h, ROWS, stride=HEADS), :
+        ].astype(jnp.bfloat16)
+
+    pl.semaphore_wait(pltpu.get_barrier_semaphore(), 11 + 2 * ((core + low) % 2))
 
     def q_push(d):
-        return remote(q_hbm, qbuf.at[NX - d], q_ss.at[d - 1], q_rs.at[NX - d - 1], at_x(d))
+        return remote(
+            qbuf.at[0], qbuf.at[NX - d], q_ss.at[d - 1], q_rs.at[NX - d - 1], at_x(d)
+        )
 
     k_push = [
-        remote(k_hbm, kbuf.at[s], k_ss.at[0], k_rs.at[0], at_s(s1)),
-        remote(k_hbm, kbuf.at[s], k_ss.at[1], k_rs.at[1], at_s(s2)),
+        remote(kbuf.at[s], kbuf.at[s], k_ss.at[0], k_rs.at[0], at_s(s1)),
+        remote(kbuf.at[s], kbuf.at[s], k_ss.at[1], k_rs.at[1], at_s(s2)),
         remote(kbuf.at[s2], kbuf.at[s2], k_ss.at[2], k_rs.at[2], at_s(s1)),
     ]
     v_push = [
-        remote(vt_hbm, vbuf.at[s], v_ss.at[0], v_rs.at[0], at_s(s1)),
-        remote(vt_hbm, vbuf.at[s], v_ss.at[1], v_rs.at[1], at_s(s2)),
+        remote(vbuf.at[s], vbuf.at[s], v_ss.at[0], v_rs.at[0], at_s(s1)),
+        remote(vbuf.at[s], vbuf.at[s], v_ss.at[1], v_rs.at[1], at_s(s2)),
         remote(vbuf.at[s2], vbuf.at[s2], v_ss.at[2], v_rs.at[2], at_s(s1)),
     ]
-    k_push[0].start()
     q_push(1).start()
     q_push(3).start()
+    k_push[0].start()
     v_push[0].start()
     k_push[1].start()
     v_push[1].start()
+
+    half_rows = pl.ds(pl.multiple_of(core * 512, 512), 512)
+
+    def wy_push(t):
+        return remote(
+            w_hbm.at[:, t * 256:(t + 1) * 256],
+            w_all.at[2 * x + far, pl.ds(pl.multiple_of(low * 512, 512), 512)],
+            wy_ss.at[t], wy_rs.at[far], at_w(t),
+        )
+
+    def wy_keep(t):
+        return pltpu.make_async_copy(
+            w_hbm.at[:, t * 256:(t + 1) * 256],
+            w_all.at[2 * x + far, pl.ds(pl.multiple_of(low * 512, 512), 512)],
+            loc_sem.at[3],
+        )
+
+    def each_wy(act, keep):
+        for t in (0, 1):
+            itself = jnp.logical_and(core == low, far == t)
+
+            @pl.when(itself)
+            def _():
+                keep(t)
+
+            @pl.when(jnp.logical_not(itself))
+            def _():
+                act(t)
+
+    def wy_arrival(t):
+        piece = w_all.at[2 * x + t, half_rows]
+        return remote(piece, piece, wy_ss.at[t], wy_rs.at[t], at_w(t))
+
+    def w_piece(chunk):
+        return w_all.at[chunk, half_rows]
+
+    def wx_push(way, g):
+        n = way * 2 + g
+        piece = w_piece(2 * x + g)
+        return remote(piece, piece, wx_ss.at[n], wx_rs.at[n], at_x(1 if way == 0 else 3))
+
+    def wf_push(way):
+        origin = (x + (3 if way == 0 else 1)) % NX
+        piece = w_piece(2 * origin + way)
+        return remote(piece, piece, wf_ss.at[way], wf_rs.at[way], at_x(1 if way == 0 else 3))
+
+    def wc_push(chunk):
+        piece = w_piece(chunk)
+        return remote(piece, piece, wc_ss.at[chunk], wc_rs.at[chunk], at_s(s1))
+
+    def wc_arrival(chunk):
+        piece = w_all.at[chunk, pl.ds(pl.multiple_of((1 - core) * 512, 512), 512)]
+        return remote(piece, piece, wc_ss.at[chunk], wc_rs.at[chunk], at_s(s1))
 
     qd[...] = jnp.zeros_like(qd)
     qd[0:HEADS, :] = probe_ref[...]
@@ -136,8 +227,8 @@
     def q_at(i):
         phase, n = i // 4, i % 4
         near = n + n // 2 - 2 * (n // 3)
-        far = 2 - n + 3 * (n // 2) - 2 * (n // 3)
-        return near * (1 - phase) + far * phase
+        there = 2 - n + 3 * (n // 2) - 2 * (n // 3)
+        return near * (1 - phase) + there * phase
 
     def k_at(i):
         phase = i // 4
@@ -158,8 +249,6 @@
             st_send.at[d - 1], st_recv.at[NX - d - 1], t_ss.at[d - 1], t_rs.at[NX - d - 1], at_x(d)
         )
 
-    for copy in own:
-        copy.wait()
     highest = lowest
     for j in range(KEYS // PIECE):
         highest = scores(0, 0, s, j, highest)
@@ -202,6 +291,19 @@
             v_push[2].start()
 
         highest = unit(1, q, kb, highest, (q_at(i + 1), k_at(i + 1)[0]))
+
+        @pl.when(i == 0)
+        def _():
+            each_wy(lambda t: wy_push(t).start(), lambda t: wy_keep(t).start())
+
+        @pl.when(i == 2)
+        def _():
+            each_wy(lambda t: wy_arrival(t).wait_recv(), lambda t: wy_keep(t).wait())
+            for g in (0, 1):
+                wx_push(0, g).start()
+                wx_push(1, g).start()
+            wc_push(2 * x).start()
+            wc_push(2 * x + 1).start()
 
         @pl.when(i >= 4)
         def _():
@@ -211,6 +313,16 @@
                 st_send[q - 1, t:t + 1, :] = lse
             o_push(q).start()
             t_push(q).start()
+
+        @pl.when(i == 6)
+        def _():
+            for way in (0, 1):
+                origin = (x + (3 if way == 0 else 1)) % NX
+                wx_push(way, way).wait_recv()
+                wf_push(way).start()
+                wx_push(way, 1 - way).wait_recv()
+                wc_push(2 * origin).start()
+                wc_push(2 * origin + 1).start()
 
         return highest
 
@@ -258,7 +370,21 @@
             total = total + o_recv[d, :, cols].astype(jnp.float32) * weight
             norm = norm + weight
         h, r = t // 2, (t % 2) * 128
-        a_ref[r:r + 128, h * HD:(h + 1) * HD] = jnp.transpose(total / norm).astype(jnp.bfloat16)
+        abuf[0, low, r:r + 128, h * HD:(h + 1) * HD] = jnp.transpose(total / norm).astype(
+            jnp.bfloat16
+        )
+
+    a_push = [
+        remote(abuf.at[0, low], abuf.at[0, low], a_ss.at[0], a_rs.at[0], at_low(s)),
+        remote(abuf.at[0, low], abuf.at[1, low], a_ss.at[1], a_rs.at[1], at_low(s2)),
+        remote(abuf.at[0, low], abuf.at[1, low], a_ss.at[2], a_rs.at[2], at_s(s2)),
+    ]
+    for copy in a_push:
+        copy.start()
+
+    for way in (0, 1):
+        wf_push(way).wait_recv()
+        wc_push(2 * ((x + 2) % NX) + way).start()
 
     for d in (1, 2, 3):
         d_push(d).wait_recv()
@@ -276,42 +402,114 @@
         norm = norm + d_all[d, 16:24, :] * weight
     dec_ref[...] = (total / norm)[0:HEADS].astype(jnp.bfloat16)
 
+    for chunk in range(NZ):
+        wc_arrival(chunk).wait_recv()
+
+    def term(d, r):
+        chunk = (z + d + NZ) % NZ
+        return jnp.dot(
+            abuf[r, 0], w_all[chunk, 0:512, :], preferred_element_type=jnp.float32
+        ) + jnp.dot(abuf[r, 1], w_all[chunk, 512:1024, :], preferred_element_type=jnp.float32)
+
+    def push(way, step, r):
+        n = (way * 4 + step) * 2 + r
+        return remote(
+            sbuf.at[n], rbuf.at[n], r_ss.at[n], r_rs.at[n],
+            at_z(1 if way == 0 else -1, s2 if (step == 3 and r == 1) else s),
+        )
+
+    sent = []
+
+    def send(way, step, r, value):
+        sbuf[(way * 4 + step) * 2 + r] = value.astype(jnp.bfloat16)
+        copy = push(way, step, r)
+        copy.start()
+        sent.append(copy)
+
+    def arrived(way, step, r):
+        push(way, step, r).wait_recv()
+        return rbuf[(way * 4 + step) * 2 + r].astype(jnp.float32)
+
+    a_push[0].wait_recv()
+    send(0, 0, 0, term(4, 0))
+    send(1, 1, 0, term(-3, 0))
+    a_push[1].wait_recv()
+    a_push[2].wait_recv()
+    send(1, 0, 1, term(4, 1))
+    send(0, 1, 1, term(3, 1))
+    send(0, 1, 0, term(3, 0) + arrived(0, 0, 0))
+    send(1, 1, 1, term(-3, 1) + arrived(1, 0, 1))
+    sbuf[16] = term(0, 1).astype(jnp.bfloat16)
+    other = remote(sbuf.at[16], rbuf.at[16], r_ss.at[16], r_rs.at[16], at_s(s2))
+    other.start()
+    for step in (2, 3):
+        send(1, step, 0, term(step - 4, 0) + arrived(1, step - 1, 0))
+        send(0, step, 1, term(4 - step, 1) + arrived(0, step - 1, 1))
+        send(0, step, 0, term(4 - step, 0) + arrived(0, step - 1, 0))
+        send(1, step, 1, term(step - 4, 1) + arrived(1, step - 1, 1))
+    total = term(0, 0) + arrived(1, 3, 0) + arrived(0, 3, 0)
+    y_ref[:, pl.ds(pl.multiple_of(far * 256, 256), 256)] = total.astype(jnp.bfloat16)
+    other.wait_recv()
+    total = rbuf[16].astype(jnp.float32) + arrived(0, 3, 1) + arrived(1, 3, 1)
+    y_ref[:, pl.ds(pl.multiple_of((1 - far) * 256, 256), 256)] = total.astype(jnp.bfloat16)
+
+    other.wait_send()
+    for copy in sent + a_push + k_push + v_push:
+        copy.wait_send()
     for d in (1, 2, 3):
         o_push(d).wait_send()
         t_push(d).wait_send()
         d_push(d).wait_send()
     q_push(2).wait_send()
     q_push(3).wait_send()
-    for copy in k_push + v_push:
-        copy.wait_send()
-
-
-def attention(q, k, vt, probe, pair):
+    each_wy(lambda t: wy_push(t).wait_send(), lambda t: None)
+    for way in (0, 1):
+        wx_push(way, 0).wait_send()
+        wx_push(way, 1).wait_send()
+        wf_push(way).wait_send()
+    for chunk in range(NZ):
+        wc_push(chunk).wait_send()
+
+
+def fused(q, fresh, prefix, probe, pair, w):
     dma = pltpu.SemaphoreType.DMA
+    bf16, f32 = jnp.bfloat16, jnp.float32
     return pl.pallas_call(
-        attention_kernel,
+        fused_kernel,
         out_shape=(
-            jax.ShapeDtypeStruct((ROWS, HEADS * HD), jnp.bfloat16),
-            jax.ShapeDtypeStruct((HEADS, HD), jnp.bfloat16),
+            jax.ShapeDtypeStruct((ROWS, 512), bf16),
+            jax.ShapeDtypeStruct((HEADS, HD), bf16),
         ),
         in_specs=[pl.BlockSpec(memory_space=pl.ANY)] * 3
-        + [pl.BlockSpec(memory_space=pltpu.VMEM)] * 2,
+        + [pl.BlockSpec(memory_space=pltpu.VMEM)] * 2
+        + [pl.BlockSpec(memory_space=pl.ANY)],
         out_specs=(pl.BlockSpec(memory_space=pltpu.VMEM),) * 2,
         scratch_shapes=[
-            pltpu.VMEM((NX, Q, HD), jnp.bfloat16),
-            pltpu.VMEM((NS, KEYS, HD), jnp.bfloat16),
-            pltpu.VMEM((NS, HD, KEYS), jnp.bfloat16),
-            pltpu.VMEM((NX, HD, Q), jnp.float32),
-            pltpu.VMEM((NX, 8, Q), jnp.float32),
-            pltpu.VMEM((NX, 8, Q), jnp.float32),
-            pltpu.VMEM((2, KEYS, Q), jnp.float32),
-            pltpu.VMEM((3, HD, Q), jnp.bfloat16),
-            pltpu.VMEM((3, HD, Q), jnp.bfloat16),
-            pltpu.VMEM((3, Q // 128, 128), jnp.float32),
-            pltpu.VMEM((3, Q // 128, 128), jnp.float32),
-            pltpu.VMEM((128, HD), jnp.bfloat16),
-            pltpu.VMEM((NX, 24, 128), jnp.float32),
-        ] + [dma((3,))] * 13,
+            pltpu.VMEM((2 * KEYS, HD), bf16),
+            pltpu.VMEM((Q, HD), bf16),
+            pltpu.VMEM((2 * KEYS, HD), f32),
+            pltpu.VMEM((NX, Q, HD), bf16),
+            pltpu.VMEM((NS, KEYS, HD), bf16),
+            pltpu.VMEM((NS, HD, KEYS), bf16),
+            pltpu.VMEM((NX, HD, Q), f32),
+            pltpu.VMEM((NX, 8, Q), f32),
+            pltpu.VMEM((NX, 8, Q), f32),
+            pltpu.VMEM((2, KEYS, Q), f32),
+            pltpu.VMEM((3, HD, Q), bf16),
+            pltpu.VMEM((3, HD, Q), bf16),
+            pltpu.VMEM((3, Q // 128, 128), f32),
+            pltpu.VMEM((3, Q // 128, 128), f32),
+            pltpu.VMEM((128, HD), bf16),
+            pltpu.VMEM((NX, 24, 128), f32),
+            pltpu.VMEM((NZ, 1024, 256), bf16),
+            pltpu.VMEM((2, 2, ROWS, 512), bf16),
+            pltpu.VMEM((17, ROWS, 256), bf16),
+            pltpu.VMEM((17, ROWS, 256), bf16),
+            dma((4,)),
+        ] + [dma((3,))] * 12 + [
+            dma((2,)), dma((2,)), dma((4,)), dma((4,)), dma((2,)), dma((2,)),
+            dma((NZ,)), dma((NZ,)), dma((3,)), dma((3,)), dma((17,)), dma((17,)),
+        ],
         compiler_params=pltpu.CompilerParams(
             collective_id=0, has_side_effects=True, vmem_limit_bytes=60 * 2 ** 20
         ),
@@ -319,117 +517,8 @@
             flops=4 * NX * Q * NS * KEYS * HD, bytes_accessed=4 * 2 ** 20,
             transcendentals=NX * Q * NS * KEYS,
         ),
-        name="attention",
-    )(q, k, vt, probe, pair)
-
-
-def projection_kernel(
-    a_hbm, w_hbm, y_ref,
-    abuf, wbuf, sbuf, rbuf, a_sem, w_sem, a_ss, a_rs, ss, rs,
-):
-    tp = lax.axis_index("tp")
-    z, half = tp // 2, tp % 2
-
-    def at_z(d):
-        return {"tp": ((z + d + NZ) % NZ) * 2 + half}
-
-    partner = {"tp": z * 2 + 1 - half}
-    order = [4, 3, -3, 2, -2, 1, -1, 0]
-
-    own = pltpu.make_async_copy(a_hbm, abuf.at[half], a_sem)
-    own.start()
-    blocks = {}
-    for n, d in enumerate(order):
-        chunk = (z + d + NZ) % NZ
-        blocks[d] = pltpu.make_async_copy(w_hbm.at[chunk], wbuf.at[n], w_sem.at[n])
-        blocks[d].start()
-
-    signal(partner)
-    signal(at_z(1))
-    signal(at_z(-1))
-    pl.semaphore_wait(pltpu.get_barrier_semaphore(), 3)
-
-    swap = pltpu.make_async_remote_copy(
-        src_ref=a_hbm, dst_ref=abuf.at[half], send_sem=a_ss, recv_sem=a_rs,
-        device_id=partner, device_id_type=MESH,
-    )
-    swap.start()
-    own.wait()
-    swap.wait_recv()
-
-    def term(d):
-        n = order.index(d)
-        blocks[d].wait()
-        return jnp.dot(
-            abuf[0], wbuf[n, 0:512, :], preferred_element_type=jnp.float32
-        ) + jnp.dot(abuf[1], wbuf[n, 512:1024, :], preferred_element_type=jnp.float32)
-
-    def push(way, step, part):
-        n = (way * 4 + step) * 2 + part
-        return pltpu.make_async_remote_copy(
-            src_ref=sbuf.at[n], dst_ref=rbuf.at[n], send_sem=ss.at[n], recv_sem=rs.at[n],
-            device_id=at_z(1 if way == 0 else -1), device_id_type=MESH,
-        )
-
-    sent = []
-
-    def send(way, step, part, value):
-        sbuf[(way * 4 + step) * 2 + part] = value.astype(jnp.bfloat16)
-        copy = push(way, step, part)
-        copy.start()
-        sent.append(copy)
-
-    def arrived(way, step, part):
-        push(way, step, part).wait_recv()
-        return rbuf[(way * 4 + step) * 2 + part].astype(jnp.float32)
-
-    def rows(value, part):
-        return value[part * 128:(part + 1) * 128]
-
-    y = term(4)
-    send(0, 0, 0, rows(y, 0))
-    send(1, 0, 1, rows(y, 1))
-    right, left = term(3), term(-3)
-    send(0, 1, 1, rows(right, 1))
-    send(1, 1, 0, rows(left, 0))
-    send(0, 1, 0, rows(right, 0) + arrived(0, 0, 0))
-    send(1, 1, 1, rows(left, 1) + arrived(1, 0, 1))
-    for step in (2, 3):
-        right, left = term(4 - step), term(step - 4)
-        for first in (0, 1):
-            send(0, step, 1 - first, rows(right, 1 - first) + arrived(0, step - 1, 1 - first))
-            send(1, step, first, rows(left, first) + arrived(1, step - 1, first))
-    y = term(0)
-    for part in (1, 0):
-        total = rows(y, part) + arrived(0, 3, part) + arrived(1, 3, part)
-        y_ref[part * 128:(part + 1) * 128, :] = total.astype(jnp.bfloat16)
-    swap.wait_send()
-    for copy in sent:
-        copy.wait_send()
-
-
-def projection(a, w):
-    dma = pltpu.SemaphoreType.DMA
-    return pl.pallas_call(
-        projection_kernel,
-        out_shape=jax.ShapeDtypeStruct((ROWS, 512), jnp.bfloat16),
-        in_specs=[pl.BlockSpec(memory_space=pl.ANY)] * 2,
-        out_specs=pl.BlockSpec(memory_space=pltpu.VMEM),
-        scratch_shapes=[
-            pltpu.VMEM((2, ROWS, 512), jnp.bfloat16),
-            pltpu.VMEM((NZ, 1024, 512), jnp.bfloat16),
-            pltpu.VMEM((16, 128, 512), jnp.bfloat16),
-            pltpu.VMEM((16, 128, 512), jnp.bfloat16),
-            dma, dma((NZ,)), dma, dma, dma((16,)), dma((16,)),
-        ],
-        compiler_params=pltpu.CompilerParams(
-            collective_id=1, has_side_effects=True, vmem_limit_bytes=60 * 2 ** 20
-        ),
-        cost_estimate=pl.CostEstimate(
-            flops=2 * ROWS * 1024 * 4096, bytes_accessed=9 * 2 ** 20, transcendentals=0
-        ),
-        name="projection",
-    )(a, w)
+        name="attention_and_projection",
+    )(q, fresh, prefix, probe, pair, w)
 
 
 def placement_kernel(ids_ref, member_ref, rows_hbm, out_hbm, zeros, sem):
@@ -481,26 +570,19 @@
     remaining_instance_ids,
     segment_destination_member,
 ):
-    route = []
-    inst_size, tp_size = lax.axis_size("inst"), lax.axis_size("tp")
-    for i in range(inst_size):
-        for t in range(tp_size):
-            core, low = i % 2, t % 2
-            route.append((i * tp_size + t, (i - core + low) * tp_size + t - low + core))
-    swapped = lax.ppermute(final_projection_weights, ("inst", "tp"), route)
-    weights = lax.all_gather(swapped, "inst", axis=0).reshape(NZ, 1024, 512)
     fresh = fresh_segment_pairs.reshape(ROWS * 2, HD)
     moved = lax.all_gather(fresh, "inst", axis=0, tiled=True)
-
-    q = jnp.transpose(fresh_segment_probes, (1, 0, 2)).reshape(Q, HD)
-    pairs = jnp.concatenate([earlier_stored_pairs, fresh_segment_pairs], axis=0)[:, :, 0, :]
-    a, decode_attention = attention(
-        q, pairs[:, 0], pairs[:, 1].T, emitted_token_probe, emitted_token_pair.reshape(2, HD)
+    span_hidden, decode_attention = fused(
+        fresh_segment_probes.reshape(Q, HD),
+        fresh,
+        earlier_stored_pairs.reshape(4 * ROWS * 2, HD),
+        emitted_token_probe,
+        emitted_token_pair.reshape(2, HD),
+        final_projection_weights,
     )
     cache = placement(
         remaining_instance_ids, segment_destination_member.reshape(-1), moved
     ).reshape(1, CAP * BLK, 2, 1, HD)
-    span_hidden = projection(a, weights)
     return span_hidden, cache, decode_attention
 
 

time: 196 us -> 130 us (0.66)
  the two profiles are of different devices: /device:TPU:2 before, /device:TPU:3 now
where the time goes in v2:
time: 130 us
  Pallas kernels  114 us (88%)
  between operations  14.1 us (11%)
    pallas_call x1, Pallas kernels, fused(): pl.pallas_call(fused_kernel, out_shape=(jax.ShapeDtypeStruct((ROWS, 512),...  95.7 us
    pallas_call x1, Pallas kernels, placement(): pl.pallas_call(placement_kernel, out_shape=jax.ShapeDtypeStruct((CAP * BL...  17.8 us
  transfers between devices with their start and end apart: 1, of which 0 were waited for; matrix products, arithmetic and copies ran while one was open for 0% of the time, Pallas kernels for 74%

profile of v2, /device:TPU:3, one launch (start us, length us, event | category | flops | bytes accessed | tf_op | source)
XLA Modules:
  0.0 129.6 jit_solution(15244674020468055073)
XLA Ops:
  7.2 0.0 all-gather.2.cloned.1.call-start
  7.2 0.7 all-gather.2.cloned.1.call-update
  7.9 95.7 %attention_and_projection.1 = (bf16[256,512]{1,0:T(8,128)(2,1)}, bf16[4,128]{1,0:T(4,128)(2,1)}) custom-call(bf16[1024,128]{1,0:T(8,128)(2,1)} %bitcast.13, bf16[512,128]{1,0:T(8,128)(2,1)} %bitcast.10, bf16[2048,128]{1,0:T(8,128)(2,1)} %bitcast.12, bf16[4,128]{1,0:T(4,128)(2,1)} %probe_ref.1, bf16[2,128]{1,0:T(2,128)(2,1)} %bitcast.14, bf16[512,512]{1,0:T(8,128)(2,1)} %w_hbm.1), custom_call_target="tpu_custom_call" | custom-call | flops 10737418240 | bytes 4194304 | tf_op jit(solution)/shard_map/attention_and_projection/pallas_call | solution.py:477
  103.6 0.0 copy-start
  103.6 0.0 copy-start.1
  103.6 0.0 all-gather.2.cloned.1.call-done.rows_hbm
  103.7 17.8 %placement.1 = bf16[2048,128]{1,0:T(8,128)(2,1)} custom-call(s32[8]{0:T(128)} %ids_ref.1, s32[32]{0:T(128)} %bitcast.11, bf16[8192,128]{1,0:T(8,128)(2,1)} %all-gather.2.cloned.1.call-done.rows_hbm), custom_call_target="tpu_custom_call" | custom-call | tf_op jit(solution)/shard_map/placement/pallas_call | solution.py:551
  121.5 0.0 copy-done
  121.5 0.7 copy.14
  122.2 0.0 copy-done.1
  122.2 0.6 copy.15
Async XLA Ops:
  7.2 96.5 %all-gather.2.cloned.1.call-start = ((), (), s32[]{:S(2)}) async-start(), calls=%async_computation | async-start | bytes 2228224 | tf_op jit(solution)/shard_map/all_gather | solution.py:574
  103.6 17.9 %copy-start = (bf16[256,512]{1,0:T(8,128)(2,1)S(1)}, bf16[256,512]{1,0:T(8,128)(2,1)}, u32[]{:S(2)}) copy-start(bf16[256,512]{1,0:T(8,128)(2,1)} %get-tuple-element.13) | copy-start | bytes 786436
  103.6 18.6 %copy-start.1 = (bf16[4,128]{1,0:T(4,128)(2,1)S(1)}, bf16[4,128]{1,0:T(4,128)(2,1)}, u32[]{:S(2)}) copy-start(bf16[4,128]{1,0:T(4,128)(2,1)} %get-tuple-element.15) | copy-start | bytes 3076
Sparse Core Ops, SparseCore 0:
  10.7 58.9 all-gather.1

commit v3 on v2

--- a/solution.py
+++ b/solution.py
@@ -30,11 +30,12 @@
 
 def fused_kernel(
     q_hbm, fresh_hbm, prefix_hbm, probe_ref, pair_ref, w_hbm,
-    y_ref, dec_ref,
+    y_ref, dec_ref, moved,
     raw, raw_q, stage, qbuf, kbuf, vbuf, acc, m_s, l_s, s_buf,
     o_send, o_recv, st_send, st_recv, qd, d_all, w_all, abuf, sbuf, rbuf,
     loc_sem, q_ss, q_rs, k_ss, k_rs, v_ss, v_rs, o_ss, o_rs, t_ss, t_rs, d_ss, d_rs,
     wy_ss, wy_rs, wx_ss, wx_rs, wf_ss, wf_rs, wc_ss, wc_rs, a_ss, a_rs, r_ss, r_rs,
+    cy_ss, cy_rs, cx_ss, cx_rs, cc_ss, cc_rs,
 ):
     me = lax.axis_index("inst")
     tp = lax.axis_index("tp")
@@ -118,6 +119,60 @@
         remote(vbuf.at[s], vbuf.at[s], v_ss.at[1], v_rs.at[1], at_s(s2)),
         remote(vbuf.at[s2], vbuf.at[s2], v_ss.at[2], v_rs.at[2], at_s(s1)),
     ]
+    half_rows = pl.ds(pl.multiple_of(core * 512, 512), 512)
+
+    def wy_push(t):
+        return remote(
+            w_hbm.at[:, t * 256:(t + 1) * 256],
+            w_all.at[2 * x + far, pl.ds(pl.multiple_of(low * 512, 512), 512)],
+            wy_ss.at[t], wy_rs.at[far], at_w(t),
+        )
+
+    def wy_keep(t):
+        return pltpu.make_async_copy(
+            w_hbm.at[:, t * 256:(t + 1) * 256],
+            w_all.at[2 * x + far, pl.ds(pl.multiple_of(low * 512, 512), 512)],
+            loc_sem.at[3],
+        )
+
+    def each_wy(act, keep):
+        for t in (0, 1):
+            itself = jnp.logical_and(core == low, far == t)
+
+            @pl.when(itself)
+            def _():
+                keep(t)
+
+            @pl.when(jnp.logical_not(itself))
+            def _():
+                act(t)
+
+    def wy_arrival(t):
+        piece = w_all.at[2 * x + t, half_rows]
+        return remote(piece, piece, wy_ss.at[t], wy_rs.at[t], at_w(t))
+
+    def w_piece(chunk):
+        return w_all.at[chunk, half_rows]
+
+    def wx_push(way, g):
+        n = way * 2 + g
+        piece = w_piece(2 * x + g)
+        return remote(piece, piece, wx_ss.at[n], wx_rs.at[n], at_x(1 if way == 0 else 3))
+
+    def wf_push(way):
+        origin = (x + (3 if way == 0 else 1)) % NX
+        piece = w_piece(2 * origin + way)
+        return remote(piece, piece, wf_ss.at[way], wf_rs.at[way], at_x(1 if way == 0 else 3))
+
+    def wc_push(chunk):
+        piece = w_piece(chunk)
+        return remote(piece, piece, wc_ss.at[chunk], wc_rs.at[chunk], at_s(s1))
+
+    def wc_arrival(chunk):
+        piece = w_all.at[chunk, pl.ds(pl.multiple_of((1 - core) * 512, 512), 512)]
+        return remote(piece, piece, wc_ss.at[chunk], wc_rs.at[chunk], at_s(s1))
+
+    each_wy(lambda t: wy_push(t).start(), lambda t: wy_keep(t).start())
     q_push(1).start()
     q_push(3).start()
     k_push[0].start()
@@ -125,58 +180,23 @@
     k_push[1].start()
     v_push[1].start()
 
-    half_rows = pl.ds(pl.multiple_of(core * 512, 512), 512)
-
-    def wy_push(t):
-        return remote(
-            w_hbm.at[:, t * 256:(t + 1) * 256],
-            w_all.at[2 * x + far, pl.ds(pl.multiple_of(low * 512, 512), 512)],
-            wy_ss.at[t], wy_rs.at[far], at_w(t),
-        )
-
-    def wy_keep(t):
-        return pltpu.make_async_copy(
-            w_hbm.at[:, t * 256:(t + 1) * 256],
-            w_all.at[2 * x + far, pl.ds(pl.multiple_of(low * 512, 512), 512)],
-            loc_sem.at[3],
-        )
-
-    def each_wy(act, keep):
-        for t in (0, 1):
-            itself = jnp.logical_and(core == low, far == t)
-
-            @pl.when(itself)
-            def _():
-                keep(t)
-
-            @pl.when(jnp.logical_not(itself))
-            def _():
-                act(t)
-
-    def wy_arrival(t):
-        piece = w_all.at[2 * x + t, half_rows]
-        return remote(piece, piece, wy_ss.at[t], wy_rs.at[t], at_w(t))
-
-    def w_piece(chunk):
-        return w_all.at[chunk, half_rows]
-
-    def wx_push(way, g):
-        n = way * 2 + g
-        piece = w_piece(2 * x + g)
-        return remote(piece, piece, wx_ss.at[n], wx_rs.at[n], at_x(1 if way == 0 else 3))
-
-    def wf_push(way):
-        origin = (x + (3 if way == 0 else 1)) % NX
-        piece = w_piece(2 * origin + way)
-        return remote(piece, piece, wf_ss.at[way], wf_rs.at[way], at_x(1 if way == 0 else 3))
-
-    def wc_push(chunk):
-        piece = w_piece(chunk)
-        return remote(piece, piece, wc_ss.at[chunk], wc_rs.at[chunk], at_s(s1))
-
-    def wc_arrival(chunk):
-        piece = w_all.at[chunk, pl.ds(pl.multiple_of((1 - core) * 512, 512), 512)]
-        return remote(piece, piece, wc_ss.at[chunk], wc_rs.at[chunk], at_s(s1))
+    fresh = raw.at[2048:2560]
+
+    def cy_push():
+        return remote(fresh, moved.at[me], cy_ss, cy_rs, at_s(s2))
+
+    def cx_push(n, d):
+        src = fresh if n == 0 else moved.at[x * NS + s2]
+        dst = moved.at[me] if n == 0 else moved.at[x * NS + s2]
+        i = n * 3 + d - 1
+        return remote(src, dst, cx_ss.at[i], cx_rs.at[n * 3 + NX - d - 1], at_x(d))
+
+    def cc_push(d, n):
+        block = moved.at[((x + d) % NX) * NS + (s, s2)[n]]
+        i = d * 2 + n
+        return remote(block, block, cc_ss.at[i], cc_rs.at[i], at_s(s1))
+
+    moved_own = pltpu.make_async_copy(fresh, moved.at[me], loc_sem.at[4])
 
     qd[...] = jnp.zeros_like(qd)
     qd[0:HEADS, :] = probe_ref[...]
@@ -292,11 +312,7 @@
 
         highest = unit(1, q, kb, highest, (q_at(i + 1), k_at(i + 1)[0]))
 
-        @pl.when(i == 0)
-        def _():
-            each_wy(lambda t: wy_push(t).start(), lambda t: wy_keep(t).start())
-
-        @pl.when(i == 2)
+        @pl.when(i == 1)
         def _():
             each_wy(lambda t: wy_arrival(t).wait_recv(), lambda t: wy_keep(t).wait())
             for g in (0, 1):
@@ -314,7 +330,12 @@
             o_push(q).start()
             t_push(q).start()
 
-        @pl.when(i == 6)
+        @pl.when(i == 4)
+        def _():
+            cy_push().start()
+            moved_own.start()
+
+        @pl.when(i == 5)
         def _():
             for way in (0, 1):
                 origin = (x + (3 if way == 0 else 1)) % NX
@@ -381,6 +402,12 @@
     ]
     for copy in a_push:
         copy.start()
+    cy_push().wait_recv()
+    moved_own.wait()
+    for n in (0, 1):
+        for d in (1, 3, 2):
+            cx_push(n, d).start()
+        cc_push(0, n).start()
 
     for way in (0, 1):
         wf_push(way).wait_recv()
@@ -447,12 +474,23 @@
         send(0, step, 1, term(4 - step, 1) + arrived(0, step - 1, 1))
         send(0, step, 0, term(4 - step, 0) + arrived(0, step - 1, 0))
         send(1, step, 1, term(step - 4, 1) + arrived(1, step - 1, 1))
+    for d in (1, 3, 2):
+        for n in (0, 1):
+            cx_push(n, NX - d).wait_recv()
+            cc_push(d, n).start()
     total = term(0, 0) + arrived(1, 3, 0) + arrived(0, 3, 0)
     y_ref[:, pl.ds(pl.multiple_of(far * 256, 256), 256)] = total.astype(jnp.bfloat16)
     other.wait_recv()
     total = rbuf[16].astype(jnp.float32) + arrived(0, 3, 1) + arrived(1, 3, 1)
     y_ref[:, pl.ds(pl.multiple_of((1 - far) * 256, 256), 256)] = total.astype(jnp.bfloat16)
 
+    cy_push().wait_send()
+    for n in (0, 1):
+        for d in (1, 2, 3):
+            cx_push(n, d).wait_send()
+        for d in range(NX):
+            cc_push(d, n).wait_send()
+            cc_push(d, n).wait_recv()
     other.wait_send()
     for copy in sent + a_push + k_push + v_push:
         copy.wait_send()
@@ -479,11 +517,13 @@
         out_shape=(
             jax.ShapeDtypeStruct((ROWS, 512), bf16),
             jax.ShapeDtypeStruct((HEADS, HD), bf16),
+            jax.ShapeDtypeStruct((NX * NS, 2 * ROWS, HD), bf16),
         ),
         in_specs=[pl.BlockSpec(memory_space=pl.ANY)] * 3
         + [pl.BlockSpec(memory_space=pltpu.VMEM)] * 2
         + [pl.BlockSpec(memory_space=pl.ANY)],
-        out_specs=(pl.BlockSpec(memory_space=pltpu.VMEM),) * 2,
+        out_specs=(pl.BlockSpec(memory_space=pltpu.VMEM),) * 2
+        + (pl.BlockSpec(memory_space=pl.ANY),),
         scratch_shapes=[
             pltpu.VMEM((2 * KEYS, HD), bf16),
             pltpu.VMEM((Q, HD), bf16),
@@ -505,10 +545,11 @@
             pltpu.VMEM((2, 2, ROWS, 512), bf16),
             pltpu.VMEM((17, ROWS, 256), bf16),
             pltpu.VMEM((17, ROWS, 256), bf16),
-            dma((4,)),
+            dma((5,)),
         ] + [dma((3,))] * 12 + [
             dma((2,)), dma((2,)), dma((4,)), dma((4,)), dma((2,)), dma((2,)),
             dma((NZ,)), dma((NZ,)), dma((3,)), dma((3,)), dma((17,)), dma((17,)),
+            dma, dma, dma((6,)), dma((6,)), dma((NZ,)), dma((NZ,)),
         ],
         compiler_params=pltpu.CompilerParams(
             collective_id=0, has_side_effects=True, vmem_limit_bytes=60 * 2 ** 20
@@ -521,43 +562,59 @@
     )(q, fresh, prefix, probe, pair, w)
 
 
-def placement_kernel(ids_ref, member_ref, rows_hbm, out_hbm, zeros, sem):
+def placement_kernel(
+    ids_ref, member_ref, rows_hbm, y_ref, dec_ref, out_ref, y_out, dec_out, sem
+):
     me = lax.axis_index("inst")
     size = BLK * 2
-    zeros[...] = jnp.zeros_like(zeros)
+
+    def block(b, n):
+        return pltpu.make_async_copy(
+            rows_hbm.at[pl.ds(b * size, size)], out_ref.at[pl.ds(n * size, size)], sem.at[n]
+        )
 
     def take(b, taken):
         mine = ids_ref[member_ref[b]] == me
 
         @pl.when(mine)
         def _():
-            pltpu.make_async_copy(
-                rows_hbm.at[pl.ds(b * size, size)], out_hbm.at[pl.ds(taken * size, size)], sem
-            ).start()
+            block(b, taken).start()
 
         return taken + mine.astype(jnp.int32)
 
     taken = lax.fori_loop(0, 32, take, 0)
 
     def clear(n, carry):
-        pltpu.make_async_copy(zeros, out_hbm.at[pl.ds(n * size, size)], sem).start()
+        out_ref[pl.ds(n * size, size), :] = jnp.zeros((size, HD), out_ref.dtype)
         return carry
 
     lax.fori_loop(taken, CAP, clear, 0)
-    pltpu.make_async_copy(rows_hbm.at[pl.ds(0, CAP * size)], out_hbm, sem).wait()
-
-
-def placement(ids, members, rows):
+    y_out[...] = y_ref[...]
+    dec_out[...] = dec_ref[...]
+
+    def finish(n, carry):
+        block(0, n).wait()
+        return carry
+
+    lax.fori_loop(0, taken, finish, 0)
+
+
+def placement(ids, members, rows, y, dec):
+    vmem = pl.BlockSpec(memory_space=pltpu.VMEM)
     return pl.pallas_call(
         placement_kernel,
-        out_shape=jax.ShapeDtypeStruct((CAP * BLK * 2, HD), jnp.bfloat16),
+        out_shape=(
+            jax.ShapeDtypeStruct((CAP * BLK * 2, HD), jnp.bfloat16),
+            jax.ShapeDtypeStruct(y.shape, y.dtype),
+            jax.ShapeDtypeStruct(dec.shape, dec.dtype),
+        ),
         in_specs=[pl.BlockSpec(memory_space=pltpu.SMEM)] * 2
-        + [pl.BlockSpec(memory_space=pl.ANY)],
-        out_specs=pl.BlockSpec(memory_space=pl.ANY),
-        scratch_shapes=[pltpu.VMEM((BLK * 2, HD), jnp.bfloat16), pltpu.SemaphoreType.DMA],
+        + [pl.BlockSpec(memory_space=pl.ANY), vmem, vmem],
+        out_specs=(vmem,) * 3,
+        scratch_shapes=[pltpu.SemaphoreType.DMA((CAP,))],
         compiler_params=pltpu.CompilerParams(vmem_limit_bytes=60 * 2 ** 20),
         name="placement",
-    )(ids, members, rows)
+    )(ids, members, rows, y, dec)
 
 
 def on_device(
@@ -570,20 +627,19 @@
     remaining_instance_ids,
     segment_destination_member,
 ):
-    fresh = fresh_segment_pairs.reshape(ROWS * 2, HD)
-    moved = lax.all_gather(fresh, "inst", axis=0, tiled=True)
-    span_hidden, decode_attention = fused(
+    span_hidden, decode_attention, moved = fused(
         fresh_segment_probes.reshape(Q, HD),
-        fresh,
+        fresh_segment_pairs.reshape(ROWS * 2, HD),
         earlier_stored_pairs.reshape(4 * ROWS * 2, HD),
         emitted_token_probe,
         emitted_token_pair.reshape(2, HD),
         final_projection_weights,
     )
-    cache = placement(
-        remaining_instance_ids, segment_destination_member.reshape(-1), moved
-    ).reshape(1, CAP * BLK, 2, 1, HD)
-    return span_hidden, cache, decode_attention
+    cache, span_hidden, decode_attention = placement(
+        remaining_instance_ids, segment_destination_member.reshape(-1),
+        moved.reshape(-1, HD), span_hidden, decode_attention,
+    )
+    return span_hidden, cache.reshape(1, CAP * BLK, 2, 1, HD), decode_attention
 
 
 def solution(mesh):

time: 130 us -> 102 us (0.78)
  the two profiles are of different devices: /device:TPU:3 before, /device:TPU:2 now
where the time goes in v3:
time: 102 us
  Pallas kernels  101 us (99%)
    pallas_call x1, Pallas kernels, fused(): pl.pallas_call(fused_kernel, out_shape=(jax.ShapeDtypeStruct((ROWS, 512),...  97.8 us
    pallas_call x1, Pallas kernels, placement(): pl.pallas_call(placement_kernel, out_shape=(jax.ShapeDtypeStruct((CAP * B...  3.13 us

profile of v3, /device:TPU:2, one launch (start us, length us, event | category | flops | bytes accessed | tf_op | source)
XLA Modules:
  0.0 101.6 jit_solution(11327147787486422489)
XLA Ops:
  0.6 97.8 %attention_and_projection.1 = (bf16[256,512]{1,0:T(8,128)(2,1)}, bf16[4,128]{1,0:T(4,128)(2,1)}, bf16[16,512,128]{2,1,0:T(8,128)(2,1)}) custom-call(bf16[1024,128]{1,0:T(8,128)(2,1)} %bitcast.13, bf16[512,128]{1,0:T(8,128)(2,1)} %bitcast.14, bf16[2048,128]{1,0:T(8,128)(2,1)} %bitcast.11, bf16[4,128]{1,0:T(4,128)(2,1)} %probe_ref.1, bf16[2,128]{1,0:T(2,128)(2,1)} %bitcast.15, ...), custom_call_target="tpu_custom_call" | custom-call | flops 10737418240 | bytes 4194304 | tf_op jit(solution)/shard_map/attention_and_projection/pallas_call | solution.py:515
  98.5 3.1 %placement.1 = (bf16[2048,128]{1,0:T(8,128)(2,1)}, bf16[256,512]{1,0:T(8,128)(2,1)}, bf16[4,128]{1,0:T(4,128)(2,1)}) custom-call(s32[8]{0:T(128)} %ids_ref.1, s32[32]{0:T(128)} %bitcast.10, bf16[8192,128]{1,0:T(8,128)(2,1)} %bitcast.9, bf16[256,512]{1,0:T(8,128)(2,1)} %get-tuple-element.10.y_ref, bf16[4,128]{1,0:T(4,128)(2,1)} %get-tuple-element.11.dec_ref), custom_call_target="tpu_custom_call" | custom-call | tf_op jit(solution)/shard_map/placement/pallas_call | solution.py:604

commit v4 on v3

--- a/solution.py
+++ b/solution.py
@@ -35,7 +35,7 @@
     o_send, o_recv, st_send, st_recv, qd, d_all, w_all, abuf, sbuf, rbuf,
     loc_sem, q_ss, q_rs, k_ss, k_rs, v_ss, v_rs, o_ss, o_rs, t_ss, t_rs, d_ss, d_rs,
     wy_ss, wy_rs, wx_ss, wx_rs, wf_ss, wf_rs, wc_ss, wc_rs, a_ss, a_rs, r_ss, r_rs,
-    cy_ss, cy_rs, cx_ss, cx_rs, cc_ss, cc_rs,
+    cy_ss, cy_rs, cx_ss, cx_rs, cc_ss, cc_rs, qf_ss, qf_rs,
 ):
     me = lax.axis_index("inst")
     tp = lax.axis_index("tp")
@@ -72,7 +72,7 @@
         pltpu.make_async_copy(fresh_hbm, raw.at[2048:2560], loc_sem.at[1]),
         pltpu.make_async_copy(q_hbm, raw_q, loc_sem.at[2]),
     ]
-    for copy in load:
+    for copy in (load[2], load[0], load[1]):
         copy.start()
 
     for d in (1, 2, 3):
@@ -90,12 +90,7 @@
         signal(at_w(0))
         signal(at_w(1))
 
-    load[0].wait()
-    load[1].wait()
-    stage[...] = raw[...].astype(jnp.float32)
-    kbuf[s] = stage[pl.ds(0, KEYS, stride=2), :].astype(jnp.bfloat16)
     load[2].wait()
-    vbuf[s] = jnp.transpose(stage[pl.ds(1, KEYS, stride=2), :]).astype(jnp.bfloat16)
     stage[0:Q] = raw_q[...].astype(jnp.float32)
     for h in range(HEADS):
         qbuf[0, h * ROWS:(h + 1) * ROWS, :] = stage[
@@ -107,6 +102,13 @@
     def q_push(d):
         return remote(
             qbuf.at[0], qbuf.at[NX - d], q_ss.at[d - 1], q_rs.at[NX - d - 1], at_x(d)
+        )
+
+    def q_forward(way):
+        part = pl.ds(way * (Q // 2), Q // 2)
+        return remote(
+            qbuf.at[3 if way == 0 else 1, part], qbuf.at[2, part],
+            qf_ss.at[way], qf_rs.at[way], at_x(1 if way == 0 else 3),
         )
 
     k_push = [
@@ -172,12 +174,16 @@
         piece = w_all.at[chunk, pl.ds(pl.multiple_of((1 - core) * 512, 512), 512)]
         return remote(piece, piece, wc_ss.at[chunk], wc_rs.at[chunk], at_s(s1))
 
-    each_wy(lambda t: wy_push(t).start(), lambda t: wy_keep(t).start())
     q_push(1).start()
     q_push(3).start()
+    load[0].wait()
+    load[1].wait()
+    stage[...] = raw[...].astype(jnp.float32)
+    kbuf[s] = stage[pl.ds(0, KEYS, stride=2), :].astype(jnp.bfloat16)
     k_push[0].start()
+    k_push[1].start()
+    vbuf[s] = jnp.transpose(stage[pl.ds(1, KEYS, stride=2), :]).astype(jnp.bfloat16)
     v_push[0].start()
-    k_push[1].start()
     v_push[1].start()
 
     fresh = raw.at[2048:2560]
@@ -291,17 +297,15 @@
 
         @pl.when(i == 0)
         def _():
-            q_push(1).wait_send()
-            q_push(2).start()
             q_push(3).wait_recv()
-
-        @pl.when(i == 1)
-        def _():
+            q_forward(1).start()
             q_push(1).wait_recv()
+            q_forward(0).start()
 
         @pl.when(i == 2)
         def _():
-            q_push(2).wait_recv()
+            q_forward(0).wait_recv()
+            q_forward(1).wait_recv()
 
         @pl.when(i == 3)
         def _():
@@ -313,6 +317,10 @@
         highest = unit(1, q, kb, highest, (q_at(i + 1), k_at(i + 1)[0]))
 
         @pl.when(i == 1)
+        def _():
+            each_wy(lambda t: wy_push(t).start(), lambda t: wy_keep(t).start())
+
+        @pl.when(i == 3)
         def _():
             each_wy(lambda t: wy_arrival(t).wait_recv(), lambda t: wy_keep(t).wait())
             for g in (0, 1):
@@ -335,7 +343,7 @@
             cy_push().start()
             moved_own.start()
 
-        @pl.when(i == 5)
+        @pl.when(i == 6)
         def _():
             for way in (0, 1):
                 origin = (x + (3 if way == 0 else 1)) % NX
@@ -402,17 +410,6 @@
     ]
     for copy in a_push:
         copy.start()
-    cy_push().wait_recv()
-    moved_own.wait()
-    for n in (0, 1):
-        for d in (1, 3, 2):
-            cx_push(n, d).start()
-        cc_push(0, n).start()
-
-    for way in (0, 1):
-        wf_push(way).wait_recv()
-        wc_push(2 * ((x + 2) % NX) + way).start()
-
     for d in (1, 2, 3):
         d_push(d).wait_recv()
     query = qd[0:8, :].astype(jnp.float32)
@@ -429,17 +426,29 @@
         norm = norm + d_all[d, 16:24, :] * weight
     dec_ref[...] = (total / norm)[0:HEADS].astype(jnp.bfloat16)
 
-    for chunk in range(NZ):
-        wc_arrival(chunk).wait_recv()
+    for way in (0, 1):
+        wf_push(way).wait_recv()
+        wc_push(2 * ((x + 2) % NX) + way).start()
+    cy_push().wait_recv()
+    moved_own.wait()
+    for n in (0, 1):
+        for d in (1, 3, 2):
+            cx_push(n, d).start()
+        cc_push(0, n).start()
+
+    present = set()
 
     def term(d, r):
         chunk = (z + d + NZ) % NZ
+        if d not in present:
+            present.add(d)
+            wc_arrival(chunk).wait_recv()
         return jnp.dot(
             abuf[r, 0], w_all[chunk, 0:512, :], preferred_element_type=jnp.float32
         ) + jnp.dot(abuf[r, 1], w_all[chunk, 512:1024, :], preferred_element_type=jnp.float32)
 
-    def push(way, step, r):
-        n = (way * 4 + step) * 2 + r
+    def push(way, step, r, p):
+        n = (way * 4 + step) * 4 + r * 2 + p
         return remote(
             sbuf.at[n], rbuf.at[n], r_ss.at[n], r_rs.at[n],
             at_z(1 if way == 0 else -1, s2 if (step == 3 and r == 1) else s),
@@ -447,42 +456,55 @@
 
     sent = []
 
-    def send(way, step, r, value):
-        sbuf[(way * 4 + step) * 2 + r] = value.astype(jnp.bfloat16)
-        copy = push(way, step, r)
-        copy.start()
-        sent.append(copy)
-
-    def arrived(way, step, r):
-        push(way, step, r).wait_recv()
-        return rbuf[(way * 4 + step) * 2 + r].astype(jnp.float32)
+    def send(way, step, r, value, add):
+        for p in (0, 1):
+            part = value[p * 128:(p + 1) * 128]
+            if add:
+                part = part + arrived(way, step - 1, r, p)
+            sbuf[(way * 4 + step) * 4 + r * 2 + p] = part.astype(jnp.bfloat16)
+            copy = push(way, step, r, p)
+            copy.start()
+            sent.append(copy)
+
+    def arrived(way, step, r, p):
+        push(way, step, r, p).wait_recv()
+        return rbuf[(way * 4 + step) * 4 + r * 2 + p].astype(jnp.float32)
 
     a_push[0].wait_recv()
-    send(0, 0, 0, term(4, 0))
-    send(1, 1, 0, term(-3, 0))
+    send(0, 0, 0, term(4, 0), False)
+    send(1, 1, 0, term(-3, 0), False)
     a_push[1].wait_recv()
     a_push[2].wait_recv()
-    send(1, 0, 1, term(4, 1))
-    send(0, 1, 1, term(3, 1))
-    send(0, 1, 0, term(3, 0) + arrived(0, 0, 0))
-    send(1, 1, 1, term(-3, 1) + arrived(1, 0, 1))
-    sbuf[16] = term(0, 1).astype(jnp.bfloat16)
-    other = remote(sbuf.at[16], rbuf.at[16], r_ss.at[16], r_rs.at[16], at_s(s2))
-    other.start()
+    send(1, 0, 1, term(4, 1), False)
+    send(0, 1, 1, term(3, 1), False)
+    send(0, 1, 0, term(3, 0), True)
+    send(1, 1, 1, term(-3, 1), True)
+    last_term = term(0, 1)
+    others = []
+    for p in (0, 1):
+        n = 32 + p
+        sbuf[n] = last_term[p * 128:(p + 1) * 128].astype(jnp.bfloat16)
+        others.append(remote(sbuf.at[n], rbuf.at[n], r_ss.at[n], r_rs.at[n], at_s(s2)))
+        others[p].start()
     for step in (2, 3):
-        send(1, step, 0, term(step - 4, 0) + arrived(1, step - 1, 0))
-        send(0, step, 1, term(4 - step, 1) + arrived(0, step - 1, 1))
-        send(0, step, 0, term(4 - step, 0) + arrived(0, step - 1, 0))
-        send(1, step, 1, term(step - 4, 1) + arrived(1, step - 1, 1))
+        send(1, step, 0, term(step - 4, 0), True)
+        send(0, step, 1, term(4 - step, 1), True)
+        send(0, step, 0, term(4 - step, 0), True)
+        send(1, step, 1, term(step - 4, 1), True)
     for d in (1, 3, 2):
         for n in (0, 1):
             cx_push(n, NX - d).wait_recv()
             cc_push(d, n).start()
-    total = term(0, 0) + arrived(1, 3, 0) + arrived(0, 3, 0)
-    y_ref[:, pl.ds(pl.multiple_of(far * 256, 256), 256)] = total.astype(jnp.bfloat16)
-    other.wait_recv()
-    total = rbuf[16].astype(jnp.float32) + arrived(0, 3, 1) + arrived(1, 3, 1)
-    y_ref[:, pl.ds(pl.multiple_of((1 - far) * 256, 256), 256)] = total.astype(jnp.bfloat16)
+    last_term = term(0, 0)
+    for p in (0, 1):
+        rows = slice(p * 128, (p + 1) * 128)
+        total = last_term[rows] + arrived(1, 3, 0, p) + arrived(0, 3, 0, p)
+        y_ref[rows, pl.ds(pl.multiple_of(far * 256, 256), 256)] = total.astype(jnp.bfloat16)
+    for p in (0, 1):
+        rows = slice(p * 128, (p + 1) * 128)
+        others[p].wait_recv()
+        total = rbuf[32 + p].astype(jnp.float32) + arrived(0, 3, 1, p) + arrived(1, 3, 1, p)
+        y_ref[rows, pl.ds(pl.multiple_of((1 - far) * 256, 256), 256)] = total.astype(jnp.bfloat16)
 
     cy_push().wait_send()
     for n in (0, 1):
@@ -491,15 +513,16 @@
         for d in range(NX):
             cc_push(d, n).wait_send()
             cc_push(d, n).wait_recv()
-    other.wait_send()
-    for copy in sent + a_push + k_push + v_push:
+    for copy in sent + others + a_push + k_push + v_push:
         copy.wait_send()
     for d in (1, 2, 3):
         o_push(d).wait_send()
         t_push(d).wait_send()
         d_push(d).wait_send()
-    q_push(2).wait_send()
+    q_push(1).wait_send()
     q_push(3).wait_send()
+    q_forward(0).wait_send()
+    q_forward(1).wait_send()
     each_wy(lambda t: wy_push(t).wait_send(), lambda t: None)
     for way in (0, 1):
         wx_push(way, 0).wait_send()
@@ -543,13 +566,13 @@
             pltpu.VMEM((NX, 24, 128), f32),
             pltpu.VMEM((NZ, 1024, 256), bf16),
             pltpu.VMEM((2, 2, ROWS, 512), bf16),
-            pltpu.VMEM((17, ROWS, 256), bf16),
-            pltpu.VMEM((17, ROWS, 256), bf16),
+            pltpu.VMEM((34, 128, 256), bf16),
+            pltpu.VMEM((34, 128, 256), bf16),
             dma((5,)),
         ] + [dma((3,))] * 12 + [
             dma((2,)), dma((2,)), dma((4,)), dma((4,)), dma((2,)), dma((2,)),
-            dma((NZ,)), dma((NZ,)), dma((3,)), dma((3,)), dma((17,)), dma((17,)),
-            dma, dma, dma((6,)), dma((6,)), dma((NZ,)), dma((NZ,)),
+            dma((NZ,)), dma((NZ,)), dma((3,)), dma((3,)), dma((34,)), dma((34,)),
+            dma, dma, dma((6,)), dma((6,)), dma((NZ,)), dma((NZ,)), dma((2,)), dma((2,)),
         ],
         compiler_params=pltpu.CompilerParams(
             collective_id=0, has_side_effects=True, vmem_limit_bytes=60 * 2 ** 20

time: 102 us -> 96.3 us (0.944)
  Pallas kernels: 101 us -> 95.4 us
    pallas_call x1, Pallas kernels: 97.8 us -> 92.3 us  [fused(): pl.pallas_call(fused_kernel, out_shape=(jax.ShapeDtypeStruct((ROWS, 512),...]
where the time goes in v4:
time: 96.3 us; the launch traced here: 96 us
  Pallas kernels  95.4 us (99%)
    pallas_call x1, Pallas kernels, fused(): pl.pallas_call(fused_kernel, out_shape=(jax.ShapeDtypeStruct((ROWS, 512),...  92.3 us
    pallas_call x1, Pallas kernels, placement(): pl.pallas_call(placement_kernel, out_shape=(jax.ShapeDtypeStruct((CAP * B...  3.11 us

profile of v4, /device:TPU:2, one launch (start us, length us, event | category | flops | bytes accessed | tf_op | source)
XLA Modules:
  0.0 96.0 jit_solution(12172372251775313112)
XLA Ops:
  0.6 92.3 %attention_and_projection.1 = (bf16[256,512]{1,0:T(8,128)(2,1)}, bf16[4,128]{1,0:T(4,128)(2,1)}, bf16[16,512,128]{2,1,0:T(8,128)(2,1)}) custom-call(bf16[1024,128]{1,0:T(8,128)(2,1)} %bitcast.13, bf16[512,128]{1,0:T(8,128)(2,1)} %bitcast.14, bf16[2048,128]{1,0:T(8,128)(2,1)} %bitcast.11, bf16[4,128]{1,0:T(4,128)(2,1)} %probe_ref.1, bf16[2,128]{1,0:T(2,128)(2,1)} %bitcast.15, ...), custom_call_target="tpu_custom_call" | custom-call | flops 10737418240 | bytes 4194304 | tf_op jit(solution)/shard_map/attention_and_projection/pallas_call | solution.py:538
  92.9 3.1 %placement.1 = (bf16[2048,128]{1,0:T(8,128)(2,1)}, bf16[256,512]{1,0:T(8,128)(2,1)}, bf16[4,128]{1,0:T(4,128)(2,1)}) custom-call(s32[8]{0:T(128)} %ids_ref.1, s32[32]{0:T(128)} %bitcast.10, bf16[8192,128]{1,0:T(8,128)(2,1)} %bitcast.9, bf16[256,512]{1,0:T(8,128)(2,1)} %get-tuple-element.10.y_ref, bf16[4,128]{1,0:T(4,128)(2,1)} %get-tuple-element.11.dec_ref), custom_call_target="tpu_custom_call" | custom-call | tf_op jit(solution)/shard_map/placement/pallas_call | solution.py:627

commit v5 on v4

--- a/solution.py
+++ b/solution.py
@@ -283,24 +283,12 @@
         q = q_at(i)
         ka, kb = k_at(i)
 
-        @pl.when(i == 0)
-        def _():
-            k_push[0].wait_recv()
-            v_push[0].wait_recv()
-
         @pl.when(i == 4)
         def _():
             k_push[2].wait_recv()
             v_push[2].wait_recv()
 
         highest = unit(0, q, ka, highest, (q, kb))
-
-        @pl.when(i == 0)
-        def _():
-            q_push(3).wait_recv()
-            q_forward(1).start()
-            q_push(1).wait_recv()
-            q_forward(0).start()
 
         @pl.when(i == 2)
         def _():
@@ -355,7 +343,18 @@
 
         return highest
 
-    highest = lax.fori_loop(0, 7, pair, highest)
+    k_push[0].wait_recv()
+    v_push[0].wait_recv()
+    highest = unit(0, 0, s, highest, (0, s1))
+    unit(1, 0, s1, highest, None)
+    q_push(3).wait_recv()
+    q_forward(1).start()
+    q_push(1).wait_recv()
+    q_forward(0).start()
+    highest = lowest
+    for j in range(KEYS // PIECE):
+        highest = scores(0, 1, s, j, highest)
+    highest = lax.fori_loop(1, 7, pair, highest)
     highest = unit(0, 0, s2, highest, (0, s3))
     unit(1, 0, s3, highest, None)
 

time: 96.3 us -> 96.1 us (level); the launches traced: 96 us -> 94.9 us
  Pallas kernels: 95.4 us -> 94.1 us
where the time goes in v5:
time: 96.1 us; the launch traced here: 94.9 us
  Pallas kernels  94.1 us (98%)
    pallas_call x1, Pallas kernels, fused(): pl.pallas_call(fused_kernel, out_shape=(jax.ShapeDtypeStruct((ROWS, 512),...  91.7 us
    pallas_call x1, Pallas kernels, placement(): pl.pallas_call(placement_kernel, out_shape=(jax.ShapeDtypeStruct((CAP * B...  2.37 us

profile of v5, /device:TPU:2, one launch (start us, length us, event | category | flops | bytes accessed | tf_op | source)
XLA Modules:
  0.0 94.9 jit_solution(1596193423411800035)
XLA Ops:
  0.6 91.7 %attention_and_projection.1 = (bf16[256,512]{1,0:T(8,128)(2,1)}, bf16[4,128]{1,0:T(4,128)(2,1)}, bf16[16,512,128]{2,1,0:T(8,128)(2,1)}) custom-call(bf16[1024,128]{1,0:T(8,128)(2,1)} %bitcast.13, bf16[512,128]{1,0:T(8,128)(2,1)} %bitcast.14, bf16[2048,128]{1,0:T(8,128)(2,1)} %bitcast.11, bf16[4,128]{1,0:T(4,128)(2,1)} %probe_ref.1, bf16[2,128]{1,0:T(2,128)(2,1)} %bitcast.15, ...), custom_call_target="tpu_custom_call" | custom-call | flops 10737418240 | bytes 4194304 | tf_op jit(solution)/shard_map/attention_and_projection/pallas_call | solution.py:537
  92.3 2.4 %placement.1 = (bf16[2048,128]{1,0:T(8,128)(2,1)}, bf16[256,512]{1,0:T(8,128)(2,1)}, bf16[4,128]{1,0:T(4,128)(2,1)}) custom-call(s32[8]{0:T(128)} %ids_ref.1, s32[32]{0:T(128)} %bitcast.10, bf16[8192,128]{1,0:T(8,128)(2,1)} %bitcast.9, bf16[256,512]{1,0:T(8,128)(2,1)} %get-tuple-element.10.y_ref, bf16[4,128]{1,0:T(4,128)(2,1)} %get-tuple-element.11.dec_ref), custom_call_target="tpu_custom_call" | custom-call | tf_op jit(solution)/shard_map/placement/pallas_call | solution.py:626
